TPU v7x, 128 devices: a whole 4x4x4 slice. The times are simulated.
128 devices in a mesh: dev: 128 (over z, y, x, core).
Axes of the slice: x: 4, y: 4, z: 4, core: 2. Of those that a mesh axis runs over, the one named last changes fastest.
Arguments:
- state: float32 [16384, 16, 512], P('dev'), may hold values from -6 to 6
- winds: float32 [2, 16384, 16, 128], P(None, 'dev'), may hold values from -3 to 3
- neighbours: int32 [16384, 8], P('dev'), may hold values from 0 to 16383, as said below
- valence: int32 [16384, 4], P('dev'), may hold values from 3 to 4, as said below
- cost: int32 [16384, 16], P('dev'), may hold values from 1 to 4, as said below
- w_in: bfloat16 [512, 384], replicated, may hold values from -0.375 to 0.375
- w_mid: bfloat16 [3, 384, 384], replicated, may hold values from -0.4375 to 0.4375
- w_out: bfloat16 [384, 512], replicated, may hold values from -0.625 to 0.625
Outputs:
- dyn_tend: float32 [16384, 16, 512], P('dev')
- phys_tend: bfloat16 [16384, 16, 512], P('dev')
Inputs may be any that keep to these rules, and one draw needn't show every extreme that they name: Row g lists the curve positions of element g's neighbours across its +a, -a, +b, -b edges and at its (+a,+b), (+a,-b), (-a,+b), (-a,-b) corners. The curve is cut into sweeps of 16 consecutive positions starting at multiples of 16; the +b and -b neighbours lie in g's own sweep, the +a neighbour and the (+a,+b), (+a,-b) corner neighbours in the next sweep, the -a neighbour and the (-a,+b), (-a,-b) corner neighbours in the previous sweep, cyclically over 16384. The elements form a closed grid of quadrilaterals without rotations: an element is its neighbour's opposite neighbour. `valence`: corners in the order of the corner neighbours; all elements around one corner point agree. `cost`: regions of 128 consecutive elements along the curve share one cloud regime.
All inputs are finite; a program needn't handle non-finite values.
Results may differ from a plain program's by a relative error of at most 0.02.
Values may be sent and summed in bfloat16 or wider, within the bound.
No kernel may reach another device: no remote copies, remote signals or barrier semaphores. Data moves between devices by JAX's collectives and lax.ppermute only.
A program may use at most 192 MiB of HBM per device.

v0:
```python
import jax
import jax.numpy as jnp
import numpy as np
from jax import lax
from jax.experimental import pallas as pl
from jax.experimental.pallas import tpu as pltpu
from jax.sharding import PartitionSpec as P

RIB = 16
SWEEPS = 8
ALL = 16384
F32 = jnp.float32
BF16 = jnp.bfloat16


def lobatto_table():
    nodes = np.array([-1.0, -1.0 / np.sqrt(5.0), 1.0 / np.sqrt(5.0), 1.0])
    weights = np.array(
        [
            1.0 / np.prod([nodes[outer] - nodes[inner] for inner in range(4) if inner != outer])
            for outer in range(4)
        ]
    )
    deriv = np.zeros((4, 4))
    for outer in range(4):
        for inner in range(4):
            if inner != outer:
                deriv[outer, inner] = weights[inner] / weights[outer] / (nodes[outer] - nodes[inner])
        deriv[outer, outer] = -np.sum(deriv[outer])
    return deriv.astype(np.float32)


def constant_table():
    deriv = lobatto_table()
    sub = np.arange(8)
    half, along = sub // 4, sub % 4
    rows = []
    for t in range(2):
        i = 2 * t + half
        for source in (half, 1 - half, 2 + half, 3 - half):
            rows.append(-deriv[i, source])
    for shift in range(4):
        rows.append(-deriv[along, (along + shift) % 4])
    for t in range(2):
        first, second = (0, 3) if t == 0 else (4, 7)
        edge = np.ones(8)
        edge += (half == t) * 1.0
        edge += (along == 0) * 1.0
        edge += (along == 3) * 1.0
        for pattern in range(4):
            present = np.zeros(8)
            present[first] = pattern // 2
            present[second] = pattern % 2
            rows.append(1.0 / (edge + present))
            rows.append(present / (edge + present))
    table = np.stack(rows).astype(np.float32)
    return np.ascontiguousarray(np.broadcast_to(table[:, :, None], table.shape + (128,)))


TABLE = constant_table()
A_AT, B_AT, W_AT = 0, 8, 12


def dot(a, b):
    return jnp.dot(a, b, preferred_element_type=F32)


def silu_half(h):
    return (h + h * jnp.tanh(h)).astype(BF16)


def sublanes():
    return lax.broadcasted_iota(jnp.int32, (8, 128), 0)


def element_advect(load, wind, table, halves, emit):
    sub = sublanes()
    along = sub % 4
    for v in range(4):
        low, high = load(0, v), load(1, v)
        pieces = (low, pltpu.roll(low, 4, 0), high, pltpu.roll(high, 4, 0))
        for t in halves:
            own = (low, high)[t]
            da = pieces[0] * table[A_AT + 4 * t]
            for k in range(1, 4):
                da = da + pieces[k] * table[A_AT + 4 * t + k]
            db = own * table[B_AT]
            for shift in range(1, 4):
                turned = jnp.where(
                    along < 4 - shift, pltpu.roll(own, 8 - shift, 0), pltpu.roll(own, 4 - shift, 0)
                )
                db = db + turned * table[B_AT + shift]
            emit(t, v, wind(0, t) * da + wind(1, t) * db)


def edge_kernel(first, last, wind_first, wind_last, table, low_out, high_out):
    def run(e, _):
        for field, wind, out, t in (
            (first, wind_first, low_out, 0),
            (last, wind_last, high_out, 1),
        ):

            def emit(t, v, value, out=out):
                at = 4 * t
                out[e, :, 128 * v : 128 * (v + 1)] = value[at : at + 4]

            element_advect(
                lambda t, v, field=field: field[e, 8 * t : 8 * t + 8, 128 * v : 128 * (v + 1)],
                lambda d, t, wind=wind: wind[d, e, 8 * t : 8 * t + 8, :],
                table,
                (t,),
                emit,
            )
        return 0

    lax.fori_loop(0, RIB, run, 0, unroll=4)


def main_kernel(
    base,
    neighbours,
    valence,
    cost,
    table,
    w_in,
    w_mid,
    w_out,
    state_hbm,
    winds_hbm,
    dyn_hbm,
    phys_hbm,
    state,
    winds,
    adv,
    dyn,
    phys,
    wi,
    wm,
    in_sem,
    out_sem,
):
    def state_copy(s):
        return pltpu.make_async_copy(
            state_hbm.at[pl.ds(s * RIB, RIB)], state.at[pl.ds(s * RIB, RIB)], in_sem.at[0, s]
        )

    def winds_copy(d, s):
        return pltpu.make_async_copy(
            winds_hbm.at[d, pl.ds(s * RIB, RIB)],
            winds.at[d, pl.ds(s * RIB, RIB)],
            in_sem.at[1 + d, s],
        )

    for s in range(SWEEPS):
        state_copy(s).start()
        winds_copy(0, s).start()
        winds_copy(1, s).start()

    def arrive(s):
        state_copy(s).wait()
        winds_copy(0, s).wait()
        winds_copy(1, s).wait()

    for v in range(4):
        adv[v, : 16 * RIB, :] = jnp.zeros((16 * RIB, 128), F32)
        adv[v, 16 * RIB * (SWEEPS + 1) : 16 * RIB * (SWEEPS + 2), :] = jnp.zeros((16 * RIB, 128), F32)
    wi[...] = w_in[...] * 0.5
    for k in range(3):
        wm[k] = w_mid[k] * 0.5
    wm[3] = (dot(w_out[...], w_in[...]) * 0.5).astype(BF16)

    def advect(e, to):
        def emit(t, v, value):
            adv[v, pl.ds(pl.multiple_of(to * 16 + 8 * t, 8), 8), :] = value

        element_advect(
            lambda t, v: state[e, 8 * t : 8 * t + 8, 128 * v : 128 * (v + 1)],
            lambda d, t: winds[d, e, 8 * t : 8 * t + 8, :],
            table,
            (0, 1),
            emit,
        )

    def assemble(e):
        sub = sublanes()
        along = sub % 4
        at = [(((neighbours[e, c] - base[0] + RIB) & (ALL - 1)) * 16) for c in range(8)]
        four = [jnp.where(valence[e, c] == 4, 1, 0) for c in range(4)]
        pattern = (four[3] * 2 + four[2], four[1] * 2 + four[0])
        own_at = pl.multiple_of((e + RIB) * 16, 16)
        for t in range(2):
            weight = table[W_AT + 8 * t + 2 * pattern[t]]
            corner = table[W_AT + 8 * t + 2 * pattern[t] + 1]
            for v in range(4):

                def rows(start):
                    return adv[v, pl.ds(start, 8), :]

                if t == 0:
                    across = jnp.where(sub < 4, rows(at[1] + 12), 0.0)
                    diagonal = jnp.where(sub == 0, rows(at[7] + 15), rows(at[6] + 9))
                else:
                    across = jnp.where(sub >= 4, rows(at[0] - 4), 0.0)
                    diagonal = jnp.where(sub == 4, rows(at[5] - 1), rows(at[4] - 7))
                beside = jnp.where(
                    along == 3,
                    rows(at[2] + 8 * t - 3),
                    jnp.where(along == 0, rows(at[3] + 8 * t + 3), 0.0),
                )
                own = adv[v, pl.ds(own_at + 8 * t, 8), :]
                dyn[e, 8 * t : 8 * t + 8, 128 * v : 128 * (v + 1)] = (
                    own + across + beside
                ) * weight + diagonal * corner

    def network(first_element, costs):
        x = state[pl.ds(first_element, RIB)].reshape(16 * RIB, 512).astype(BF16)
        a = dot(x, wi[...])
        yield
        total = None
        for s in range(4):
            h = silu_half(a)
            for k in range(3):
                h = dot(h, wm[k])
                yield
                h = silu_half(h)
            wide = h.astype(F32)
            if s == 0:
                total = wide
            else:
                active = costs > s
                total = total + jnp.concatenate(
                    [
                        jnp.where(active, wide[:, 128 * v : 128 * (v + 1)], 0.0)
                        for v in range(3)
                    ],
                    1,
                )
            if s < 3:
                a = a + dot(h, wm[3])
                yield
        tend = dot(total.astype(BF16), w_out[...])
        phys[pl.ds(first_element, RIB)] = tend.astype(BF16).reshape(RIB, 16, 512)

    def column_costs(first_element):
        block = cost[pl.ds(first_element, RIB), :].astype(F32)
        spread = jnp.broadcast_to(block[:, None, :], (RIB, 16, 16))
        point = lax.broadcasted_iota(jnp.int32, (RIB, 16, 16), 1)
        lane = lax.broadcasted_iota(jnp.int32, (RIB, 16, 16), 2)
        spread = jnp.where(point == lane, spread, 0.0).reshape(16 * RIB, 16)
        return dot(spread.astype(BF16), jnp.ones((16, 128), BF16))

    def dyn_copy(t):
        return pltpu.make_async_copy(
            dyn.at[pl.ds(t * 32, 32)], dyn_hbm.at[pl.ds(t * 32, 32)], out_sem.at[0, t]
        )

    def phys_copy(t):
        return pltpu.make_async_copy(
            phys.at[pl.ds(t * 32, 32)], phys_hbm.at[pl.ds(t * 32, 32)], out_sem.at[1, t]
        )

    arrive(0)

    def first_advect(e, _):
        advect(e, e + RIB)
        return 0

    lax.fori_loop(0, RIB, first_advect, 0, unroll=4)

    def step(t, _):
        arrive(2 * t + 1)

        @pl.when(t < 3)
        def _():
            arrive(2 * t + 2)

        def fill():
            for e in range(32):
                number = t * 32 + RIB + e
                if e < RIB:
                    advect(number, number + RIB)
                else:
                    advect(
                        jnp.minimum(number, RIB * SWEEPS - RIB + e - RIB),
                        jnp.where(t == 3, RIB * (SWEEPS + 2) + e - RIB, number + RIB),
                    )
                if e % 4 == 3:
                    yield
            for e in range(32):
                assemble(t * 32 + e)
                if e % 4 == 3:
                    yield

        chains = [
            network(t * 32 + c * RIB, column_costs(t * 32 + c * RIB)) for c in range(2)
        ]
        live = chains + [fill()]
        while live:
            later = []
            for part in live:
                try:
                    next(part)
                    later.append(part)
                except StopIteration:
                    pass
            live = later
        dyn_copy(t).start()
        phys_copy(t).start()
        return 0

    lax.fori_loop(0, 4, step, 0)
    for t in range(4):
        dyn_copy(t).wait()
        phys_copy(t).wait()


def halo_kernel(
    base, neighbours, valence, table, before, after, dyn_in, dyn_hbm, low, high, sem
):
    last = RIB * (SWEEPS - 1)
    parts = (
        (low, dyn_hbm.at[pl.ds(0, RIB), pl.ds(0, 8)], 0),
        (high, dyn_hbm.at[pl.ds(last, RIB), pl.ds(8, 8)], 1),
    )
    loads = [pltpu.make_async_copy(far, near, sem.at[k]) for near, far, k in parts]
    stores = [pltpu.make_async_copy(near, far, sem.at[2 + k]) for near, far, k in parts]
    for copy in loads:
        copy.start()
    for copy in loads:
        copy.wait()
    sub = lax.broadcasted_iota(jnp.int32, (4, 512), 0)

    def wide(entry):
        return jnp.concatenate([entry] * 4, 1)

    def run(e, _):
        for near, t, halo, first in ((low, 0, before, 0), (high, 1, after, last)):
            own = e + first
            slots = (1, 7, 6) if t == 0 else (0, 5, 4)
            origin = base[0] + (RIB * SWEEPS if t else -RIB)
            at = [(neighbours[own, c] - origin) & (ALL - 1) for c in slots]
            four = [jnp.where(valence[own, c] == 4, 1, 0) for c in range(4)]
            pattern = (four[3] * 2 + four[2], four[1] * 2 + four[0])[t]
            weight = table[W_AT + 8 * t + 2 * pattern, 4 * t : 4 * t + 4, :]
            corner = table[W_AT + 8 * t + 2 * pattern + 1, 4 * t : 4 * t + 4, :]
            diagonal = jnp.where(sub == 0, halo[at[1], 3:4, :], halo[at[2], 0:1, :])
            near[e, 4 * t : 4 * t + 4, :] = (
                near[e, 4 * t : 4 * t + 4, :]
                + halo[at[0]] * wide(weight)
                + diagonal * wide(corner)
            )
        return 0

    lax.fori_loop(0, RIB, run, 0, unroll=4)
    for copy in stores:
        copy.start()
    for copy in stores:
        copy.wait()


def body(state, winds, neighbours, valence, cost, w_in, w_mid, w_out):
    vmem = pl.BlockSpec(memory_space=pltpu.VMEM)
    smem = pl.BlockSpec(memory_space=pltpu.SMEM)
    anywhere = pl.BlockSpec(memory_space=pl.ANY)
    devices = lax.axis_size("dev")
    base = (lax.axis_index("dev") * (RIB * SWEEPS)).astype(jnp.int32).reshape(1)
    table = jnp.asarray(TABLE)

    def sweep_of(which):
        return pl.BlockSpec((RIB, 16, 512), lambda i: (which, 0, 0))

    def winds_of(which):
        return pl.BlockSpec((2, RIB, 16, 128), lambda i: (0, which, 0, 0))

    edge = jax.ShapeDtypeStruct((RIB, 4, 512), F32)
    edge_spec = pl.BlockSpec((RIB, 4, 512), lambda i: (0, 0, 0))
    low, high = pl.pallas_call(
        edge_kernel,
        grid=(1,),
        out_shape=(edge, edge),
        in_specs=[
            sweep_of(0),
            sweep_of(SWEEPS - 1),
            winds_of(0),
            winds_of(SWEEPS - 1),
            pl.BlockSpec(TABLE.shape, lambda i: (0, 0, 0)),
        ],
        out_specs=(edge_spec, edge_spec),
        cost_estimate=pl.CostEstimate(
            flops=10_000_000, bytes_accessed=2_000_000, transcendentals=0
        ),
    )(state, state, winds, winds, table)
    forward = [(i, (i + 1) % devices) for i in range(devices)]
    backward = [(target, source) for source, target in forward]
    before = lax.ppermute(high, "dev", forward)
    after = lax.ppermute(low, "dev", backward)

    dyn, phys = pl.pallas_call(
        main_kernel,
        out_shape=(
            jax.ShapeDtypeStruct(state.shape, F32),
            jax.ShapeDtypeStruct(state.shape, BF16),
        ),
        in_specs=[smem, smem, smem, vmem, vmem, vmem, vmem, vmem, anywhere, anywhere],
        out_specs=(anywhere, anywhere),
        scratch_shapes=[
            pltpu.VMEM((RIB * SWEEPS, 16, 512), F32),
            pltpu.VMEM((2, RIB * SWEEPS, 16, 128), F32),
            pltpu.VMEM((4, (SWEEPS + 3) * RIB * 16, 128), F32),
            pltpu.VMEM((RIB * SWEEPS, 16, 512), F32),
            pltpu.VMEM((RIB * SWEEPS, 16, 512), BF16),
            pltpu.VMEM((512, 384), BF16),
            pltpu.VMEM((4, 384, 384), BF16),
            pltpu.SemaphoreType.DMA((3, SWEEPS)),
            pltpu.SemaphoreType.DMA((2, 4)),
        ],
        compiler_params=pltpu.CompilerParams(vmem_limit_bytes=44 * 2**20),
        cost_estimate=pl.CostEstimate(
            flops=12_000_000_000, bytes_accessed=14_000_000, transcendentals=10_000_000
        ),
    )(base, neighbours, valence, cost, table, w_in, w_mid, w_out, state, winds)

    dyn = pl.pallas_call(
        halo_kernel,
        out_shape=jax.ShapeDtypeStruct(state.shape, F32),
        in_specs=[smem, smem, smem, vmem, vmem, vmem, anywhere],
        out_specs=anywhere,
        scratch_shapes=[
            pltpu.VMEM((RIB, 8, 512), F32),
            pltpu.VMEM((RIB, 8, 512), F32),
            pltpu.SemaphoreType.DMA((4,)),
        ],
        input_output_aliases={6: 0},
        cost_estimate=pl.CostEstimate(
            flops=1_000_000, bytes_accessed=2_000_000, transcendentals=0
        ),
    )(base, neighbours, valence, table, before, after, dyn)
    return dyn, phys


def solution(mesh):
    return jax.shard_map(
        body,
        mesh=mesh,
        in_specs=(
            P("dev", None, None),
            P(None, "dev", None, None),
            P("dev", None),
            P("dev", None),
            P("dev", None),
            P(),
            P(),
            P(),
        ),
        out_specs=(P("dev", None, None), P("dev", None, None)),
        check_vma=False,
    )
```

profile of v0, /device:TPU:0, one launch (start us, length us, event | category | flops | bytes accessed | tf_op | source)
XLA Modules:
  0.0 54.9 jit_solution(6451231885131413744)
XLA Ops:
  0.6 0.0 copy-start.2
  0.6 0.0 copy-start.1
  0.7 0.0 copy-start.10
  0.7 0.0 copy-start.11
  0.7 0.0 copy-start.5
  0.7 2.7 %shard_map.104 = (f32[16,4,512]{2,1,0:T(4,128)}, f32[16,4,512]{2,1,0:T(4,128)}) custom-call(f32[128,16,512]{2,1,0:T(8,128)} %state_hbm.1, f32[128,16,512]{2,1,0:T(8,128)} %state_hbm.1, f32[2,128,16,128]{3,2,1,0:T(8,128)} %winds_hbm.1, f32[2,128,16,128]{3,2,1,0:T(8,128)} %winds_hbm.1, f32[28,8,128]{2,1,0:T(8,128)} %constant.8.clone.table), custom_call_target="tpu_custom_call" | custom-call | flops 10000000 | bytes 2000000 | tf_op jit(solution)/shard_map/pallas_call | solution.py:377
  3.4 0.0 collective-permute-start
  3.4 8.2 %collective-permute-start.1 = (f32[16,4,512]{2,1,0:T(4,128)}, f32[16,4,512]{2,1,0:T(4,128)S(1)}, u32[]{:S(2)}, u32[]{:S(2)}) collective-permute-start(f32[16,4,512]{2,1,0:T(4,128)} %get-tuple-element.7), channel_id=1, source_target_pairs={{1,0},{2,1},{3,2},{4,3},{5,4},{6,5},{7,6},{8,7},{9,8},{10,9},{11,1... | collective-permute-start | bytes 393224 | tf_op jit(solution)/shard_map/ppermute | solution.py:396
  11.6 0.0 copy-done.10
  11.6 0.1 copy.15.neighbours
  11.7 0.0 copy-done.11
  11.7 0.0 copy-start.3
  11.7 0.1 copy.16.valence
  11.8 0.0 copy-start.4
  11.9 0.8 %copy.14.cost = s32[128,16]{1,0:T(8,128)S(1)} copy(s32[128,16]{0,1:T(8,128)} %param.13) | data formatting | bytes 16384 | tf_op args[4]
  12.7 0.0 copy-done.2
  12.7 0.0 copy-done.1
  12.7 0.0 copy-done.5
  12.7 0.0 copy-start
  12.7 2.2 %copy-done = f32[128,16,512]{2,1,0:T(8,128)S(1)} copy-done((f32[128,16,512]{2,1,0:T(8,128)S(1)}, f32[128,16,512]{2,1,0:T(8,128)}, u32[]{:S(2)}) %copy-start) | copy-done | bytes 4194328
  14.9 1.0 %copy-done.6 = bf16[512,384]{1,0:T(8,128)(2,1)S(1)} copy-done((bf16[512,384]{1,0:T(8,128)(2,1)S(1)}, bf16[512,384]{1,0:T(8,128)(2,1)}, u32[]{:S(2)}) %copy-start.6) | copy-done | bytes 393240
  15.9 1.0 %copy-done.7 = bf16[384,512]{1,0:T(8,128)(2,1)S(1)} copy-done((bf16[384,512]{1,0:T(8,128)(2,1)S(1)}, bf16[384,512]{1,0:T(8,128)(2,1)}, u32[]{:S(2)}) %copy-start.7) | copy-done | bytes 393240
  16.9 32.2 %shard_map.105 = (f32[128,16,512]{2,1,0:T(8,128)}, bf16[128,16,512]{2,1,0:T(8,128)(2,1)}) custom-call(s32[1]{0:T(128)} %bitcast.base, s32[128,8]{1,0:T(8,128)S(1)} %copy.15.neighbours, s32[128,4]{1,0:T(8,128)S(1)} %copy.16.valence, s32[128,16]{1,0:T(8,128)S(1)} %copy.14.cost, f32[28,8,128]{2,1,0:T(8,128)S(1)} %copy-done.2, bf16[512,384]{1,0:T(8,128)(2,1)S(1)} %copy-done.6, ...), custom_call_target="tpu_custom_call" | custom-call | flops 12000000000 | bytes 14000000 | tf_op jit(solution)/shard_map/pallas_call | solution.py:398
  49.1 0.0 copy-done.3
  49.1 0.0 copy-done.4
  49.1 0.0 collective-permute-done.before
  49.1 0.0 copy-start.8
  49.1 0.0 collective-permute-done.1.after
  49.2 0.0 copy-start.9
  49.2 0.6 %copy-done.8 = f32[16,4,512]{2,1,0:T(4,128)} copy-done((f32[16,4,512]{2,1,0:T(4,128)}, f32[16,4,512]{2,1,0:T(4,128)S(1)}, u32[]{:S(2)}) %copy-start.8) | copy-done | bytes 131096
  49.8 0.0 copy-done.9
  49.8 5.1 %shard_map.106 = f32[128,16,512]{2,1,0:T(8,128)} custom-call(s32[1]{0:T(128)} %bitcast.base, s32[128,8]{1,0:T(8,128)} %copy-done.3, s32[128,4]{1,0:T(8,128)} %copy-done.4, f32[28,8,128]{2,1,0:T(8,128)} %constant.8.clone.table, f32[16,4,512]{2,1,0:T(4,128)} %copy-done.8, f32[16,4,512]{2,1,0:T(4,128)} %copy-done.9, ...), custom_call_target="tpu_custom_call", output_to_operand_aliasing={{}: (6, {})} | custom-call | flops 1000000 | bytes 2000000 | tf_op jit(solution)/shard_map/pallas_call | solution.py:423
  (2 shorter events, 0.0 us)
Async XLA Ops:
  0.6 12.0 %copy-start.2 = (f32[28,8,128]{2,1,0:T(8,128)S(1)}, f32[28,8,128]{2,1,0:T(8,128)}, u32[]{:S(2)}) copy-start(f32[28,8,128]{2,1,0:T(8,128)} %constant.8.clone.table) | copy-start | bytes 344068
  0.6 12.0 %copy-start.1 = (f32[2,128,16,128]{3,2,1,0:T(8,128)S(1)}, f32[2,128,16,128]{3,2,1,0:T(8,128)}, u32[]{:S(2)}) copy-start(f32[2,128,16,128]{3,2,1,0:T(8,128)} %winds_hbm.1) | copy-start | bytes 6291460
  0.7 11.0 %copy-start.10 = (s32[128,8]{0,1:T(8,128)S(1)}, s32[128,8]{0,1:T(8,128)}, u32[]{:S(2)}) copy-start(s32[128,8]{0,1:T(8,128)} %param.11) | copy-start | bytes 12292
  0.7 11.1 %copy-start.11 = (s32[128,4]{0,1:T(4,128)S(1)}, s32[128,4]{0,1:T(4,128)}, u32[]{:S(2)}) copy-start(s32[128,4]{0,1:T(4,128)} %param.12) | copy-start | bytes 6148
  0.7 12.0 %copy-start.5 = (bf16[3,384,384]{2,1,0:T(8,128)(2,1)S(1)}, bf16[3,384,384]{2,1,0:T(8,128)(2,1)}, u32[]{:S(2)}) copy-start(bf16[3,384,384]{2,1,0:T(8,128)(2,1)} %w_mid.1) | copy-start | bytes 2654212
  3.4 45.7 %collective-permute-start = (f32[16,4,512]{2,1,0:T(4,128)}, f32[16,4,512]{2,1,0:T(4,128)S(1)}, u32[]{:S(2)}, u32[]{:S(2)}) collective-permute-start(f32[16,4,512]{2,1,0:T(4,128)} %get-tuple-element.6), channel_id=1, source_target_pairs={{0,1},{1,2},{2,3},{3,4},{4,5},{5,6},{6,7},{7,8},{8,9},{9,10},{10,1... | collective-permute-start | bytes 393224 | tf_op jit(solution)/shard_map/ppermute | solution.py:395
  3.4 45.7 %collective-permute-start.1 = (f32[16,4,512]{2,1,0:T(4,128)}, f32[16,4,512]{2,1,0:T(4,128)S(1)}, u32[]{:S(2)}, u32[]{:S(2)}) collective-permute-start(f32[16,4,512]{2,1,0:T(4,128)} %get-tuple-element.7), channel_id=1, source_target_pairs={{1,0},{2,1},{3,2},{4,3},{5,4},{6,5},{7,6},{8,7},{9,8},{10,9},{11,1... | collective-permute-start | bytes 393224 | tf_op jit(solution)/shard_map/ppermute | solution.py:396
  11.7 37.4 %copy-start.3 = (s32[128,8]{1,0:T(8,128)}, s32[128,8]{1,0:T(8,128)S(1)}, u32[]{:S(2)}) copy-start(s32[128,8]{1,0:T(8,128)S(1)} %copy.15.neighbours) | copy-start | bytes 12292
  11.8 37.3 %copy-start.4 = (s32[128,4]{1,0:T(8,128)}, s32[128,4]{1,0:T(8,128)S(1)}, u32[]{:S(2)}) copy-start(s32[128,4]{1,0:T(8,128)S(1)} %copy.16.valence) | copy-start | bytes 6148
  12.7 2.2 %copy-start = (f32[128,16,512]{2,1,0:T(8,128)S(1)}, f32[128,16,512]{2,1,0:T(8,128)}, u32[]{:S(2)}) copy-start(f32[128,16,512]{2,1,0:T(8,128)} %state_hbm.1) | copy-start | bytes 12582916
  14.9 1.0 %copy-start.6 = (bf16[512,384]{1,0:T(8,128)(2,1)S(1)}, bf16[512,384]{1,0:T(8,128)(2,1)}, u32[]{:S(2)}) copy-start(bf16[512,384]{1,0:T(8,128)(2,1)} %w_in.1) | copy-start | bytes 1179652
  15.9 1.0 %copy-start.7 = (bf16[384,512]{1,0:T(8,128)(2,1)S(1)}, bf16[384,512]{1,0:T(8,128)(2,1)}, u32[]{:S(2)}) copy-start(bf16[384,512]{1,0:T(8,128)(2,1)} %w_out.1) | copy-start | bytes 1179652
  49.1 0.7 %copy-start.8 = (f32[16,4,512]{2,1,0:T(4,128)}, f32[16,4,512]{2,1,0:T(4,128)S(1)}, u32[]{:S(2)}) copy-start(f32[16,4,512]{2,1,0:T(4,128)S(1)} %collective-permute-done.before) | copy-start | bytes 393220
  49.2 0.7 %copy-start.9 = (f32[16,4,512]{2,1,0:T(4,128)}, f32[16,4,512]{2,1,0:T(4,128)S(1)}, u32[]{:S(2)}) copy-start(f32[16,4,512]{2,1,0:T(4,128)S(1)} %collective-permute-done.1.after) | copy-start | bytes 393220
where the time goes:
time: 55.4 us; the launch traced here: 54.9 us
  Pallas kernels  40 us (72%)
  starting transfers between devices  8.21 us (15%)
  local copies, waits for them, and re-layouts  5.91 us (11%)
  between operations  0.77 us (1%)
    pallas_call x1, Pallas kernels, body(): pl.pallas_call(main_kernel, out_shape=(jax.ShapeDtypeStruct(state.shape,...  32.2 us
    ppermute x1, starting transfers between devices, body(): after = lax.ppermute(low, 'dev', backward)  8.21 us
    unnamed x27, local copies, waits for them, and re-layouts  5.91 us
    pallas_call x1, Pallas kernels, body(): pl.pallas_call(halo_kernel, out_shape=jax.ShapeDtypeStruct(state.shape, F...  5.1 us
    pallas_call x1, Pallas kernels, body(): pl.pallas_call(edge_kernel, grid=(1,), out_shape=(edge, edge), in_specs=[...  2.72 us
  transfers between devices with their start and end apart: 2, of which 0 were waited for; matrix products, arithmetic and copies ran while one was open for 2% of the time, Pallas kernels for 59%

commit v1 on v0

v1 whole, which is shorter than its diff:
```python
import functools

import jax
import jax.numpy as jnp
import numpy as np
from jax import lax
from jax.experimental import pallas as pl
from jax.experimental.pallas import tpu as pltpu
from jax.sharding import PartitionSpec as P

RIB = 16
SWEEPS = 8
STEPS = 4
ALL = 16384
F32 = jnp.float32
BF16 = jnp.bfloat16


def lobatto_table():
    nodes = np.array([-1.0, -1.0 / np.sqrt(5.0), 1.0 / np.sqrt(5.0), 1.0])
    weights = np.array(
        [
            1.0 / np.prod([nodes[outer] - nodes[inner] for inner in range(4) if inner != outer])
            for outer in range(4)
        ]
    )
    deriv = np.zeros((4, 4))
    for outer in range(4):
        for inner in range(4):
            if inner != outer:
                deriv[outer, inner] = weights[inner] / weights[outer] / (nodes[outer] - nodes[inner])
        deriv[outer, outer] = -np.sum(deriv[outer])
    return deriv.astype(np.float32)


def constant_table():
    deriv = lobatto_table()
    sub = np.arange(8)
    half, along = sub // 4, sub % 4
    rows = []
    for t in range(2):
        i = 2 * t + half
        for source in (half, 1 - half, 2 + half, 3 - half):
            rows.append(-deriv[i, source])
    for shift in range(4):
        rows.append(-deriv[along, (along + shift) % 4])
    for t in range(2):
        first, second = (0, 3) if t == 0 else (4, 7)
        edge = np.ones(8)
        edge += (half == t) * 1.0
        edge += (along == 0) * 1.0
        edge += (along == 3) * 1.0
        for pattern in range(4):
            present = np.zeros(8)
            present[first] = pattern // 2
            present[second] = pattern % 2
            rows.append(1.0 / (edge + present))
            rows.append(present / (edge + present))
    table = np.stack(rows).astype(np.float32)
    return np.ascontiguousarray(np.broadcast_to(table[:, :, None], table.shape + (128,)))


TABLE = constant_table()
A_AT, B_AT, W_AT = 0, 8, 12
LAYERS = 16


def dot(a, b):
    return jnp.dot(a, b, preferred_element_type=F32)


def silu_half(h):
    h = h.astype(BF16)
    return h + h * jnp.tanh(h)


def sublanes():
    return lax.broadcasted_iota(jnp.int32, (8, 128), 0)


def turned(tile, pattern):
    return jnp.take_along_axis(tile, pattern, axis=0, mode="promise_in_bounds")


def element_advect(load, wind, table, halves, emit):
    sub = sublanes()
    swap = sub ^ 4
    shifts = [(sub & 4) | ((sub + shift) & 3) for shift in range(4)]
    for v in range(4):
        low, high = load(0, v), load(1, v)
        pieces = (low, turned(low, swap), high, turned(high, swap))
        for t in halves:
            own = (low, high)[t]
            da = pieces[0] * table[A_AT + 4 * t]
            for k in range(1, 4):
                da = da + pieces[k] * table[A_AT + 4 * t + k]
            db = own * table[B_AT]
            for shift in range(1, 4):
                db = db + turned(own, shifts[shift]) * table[B_AT + shift]
            emit(t, v, wind(0, t) * da + wind(1, t) * db)


def half_split(base):
    return 2


def main_kernel(opening, *refs):
    if opening:
        (base, neighbours, valence, cost, table, w_in, w_mid, w_out, state_hbm, winds_hbm,
         dyn_hbm, phys_hbm, edge_low, edge_high, part, plan_out, wi, wm, wo,
         state, winds, adv, dyn, phys, plan, plan_sem, w_sem, in_sem, out_sem) = refs
    else:
        (base, plan, cost, table, wi, wm, wo, state_hbm, winds_hbm, _, _,
         dyn_hbm, phys_hbm, part,
         state, winds, adv, dyn, phys, in_sem, out_sem) = refs
    middle = half_split(base[0])
    first_step, last_step = (0, middle) if opening else (middle, STEPS)

    def copies(s):
        at = pl.ds(s * RIB, RIB)
        return (
            pltpu.make_async_copy(state_hbm.at[at], state.at[at], in_sem.at[0, s]),
            pltpu.make_async_copy(winds_hbm.at[0, at], winds.at[0, at], in_sem.at[1, s]),
            pltpu.make_async_copy(winds_hbm.at[1, at], winds.at[1, at], in_sem.at[2, s]),
        )

    def fetch(s):
        for copy in copies(s):
            copy.start()

    def arrive(s):
        for copy in copies(s):
            copy.wait()

    def each(start, stop, act):
        def one(s, _):
            act(s)
            return 0

        lax.fori_loop(start, stop, one, 0)

    if opening:
        fetch(0)
        fetch(SWEEPS - 1)
        loads = [
            pltpu.make_async_copy(w_in, wi, w_sem.at[0]),
            pltpu.make_async_copy(w_mid, wm.at[pl.ds(0, 3)], w_sem.at[1]),
            pltpu.make_async_copy(w_out, wo, w_sem.at[2]),
        ]
        for copy in loads:
            copy.start()
        each(1, 2 * last_step + 1, fetch)
        rows = ((neighbours[...] - base[0] + RIB) & (ALL - 1)) * 16
        plan_out[0:8, :] = rows
        corner = valence[...] - 3
        plan_out[8:9, :] = corner[3:4] * 4 + corner[2:3] * 2 + W_AT
        plan_out[9:10, :] = corner[1:2] * 4 + corner[0:1] * 2 + W_AT + 8
        plan_out[10:16, :] = jnp.zeros((6, 128), jnp.int32)
        send_plan = pltpu.make_async_copy(plan_out, plan, plan_sem)
        send_plan.start()
    else:
        each(2 * first_step - 1, SWEEPS, fetch)

    for v in range(4):
        adv[v, : 16 * RIB, :] = jnp.zeros((16 * RIB, 128), F32)
        adv[v, 16 * RIB * (SWEEPS + 1) : 16 * RIB * (SWEEPS + 2), :] = jnp.zeros(
            (16 * RIB, 128), F32
        )
    costs = lax.dot_general(
        cost[...].astype(BF16),
        (
            lax.broadcasted_iota(jnp.int32, (16, 16), 0)
            == lax.broadcasted_iota(jnp.int32, (16, 16), 1)
        ).astype(BF16),
        (((0,), (0,)), ((), ())),
        preferred_element_type=F32,
    )

    def advect(e, to, halves=(0, 1), emit=None):
        def keep(t, v, value):
            adv[v, pl.ds(pl.multiple_of(to * 16 + 8 * t, 8), 8), :] = value
            if emit is not None:
                emit(t, v, value)

        element_advect(
            lambda t, v: state[e, 8 * t : 8 * t + 8, 128 * v : 128 * (v + 1)],
            lambda d, t: winds[d, e, 8 * t : 8 * t + 8, :],
            table,
            halves,
            keep,
        )

    def assemble(e, half=None):
        sub = sublanes()
        along = sub % 4
        at = [plan[c, e] for c in range(8)]
        own_at = pl.multiple_of((e + RIB) * 16, 16)
        for t in range(2):
            entry = plan[8 + t, e]
            weight = table[entry]
            corner = table[entry + 1]
            for v in range(4):

                def rows(start):
                    return adv[v, pl.ds(start, 8), :]

                if t == 0:
                    across = jnp.where(sub < 4, rows(at[1] + 12), 0.0)
                    diagonal = jnp.where(sub == 0, rows(at[7] + 15), rows(at[6] + 9))
                else:
                    across = jnp.where(sub >= 4, rows(at[0] - 4), 0.0)
                    diagonal = jnp.where(sub == 4, rows(at[5] - 1), rows(at[4] - 7))
                beside = jnp.where(
                    along == 3,
                    rows(at[2] + 8 * t - 3),
                    jnp.where(along == 0, rows(at[3] + 8 * t + 3), 0.0),
                )
                own = adv[v, pl.ds(own_at + 8 * t, 8), :]
                dyn[e, 8 * t : 8 * t + 8, 128 * v : 128 * (v + 1)] = (
                    own + across + beside
                ) * weight + diagonal * corner

    def network(first_element, counts):
        x = state[pl.ds(first_element, RIB)].reshape(16 * RIB, 512).astype(BF16)
        a = dot(x, wi[...])
        yield a[:8, :128]
        total = None
        for s in range(4):
            h = silu_half(a)
            for k in range(3):
                pre = dot(h, wm[k])
                yield pre[:8, :128]
                h = silu_half(pre)
            wide = h.astype(F32)
            if s == 0:
                total = wide
            else:
                active = counts > s
                total = total + jnp.concatenate(
                    [
                        jnp.where(active, wide[:, 128 * v : 128 * (v + 1)], 0.0)
                        for v in range(3)
                    ],
                    1,
                )
            if s < 3:
                a = a + dot(h, wm[3])
                yield a[:8, :128]
        tend = dot(total.astype(BF16), wo[...])
        phys[pl.ds(first_element, RIB)] = tend.astype(BF16).reshape(RIB, 16, 512)

    def column_counts(first_element):
        block = costs_ref(first_element)
        spread = jnp.broadcast_to(block[:, None, :], (RIB, 16, 16))
        point = lax.broadcasted_iota(jnp.int32, (RIB, 16, 16), 1)
        lane = lax.broadcasted_iota(jnp.int32, (RIB, 16, 16), 2)
        spread = jnp.where(point == lane, spread, 0.0).reshape(16 * RIB, 16)
        return dot(spread.astype(BF16), jnp.ones((16, 128), BF16))

    for s in range(SWEEPS):
        winds[0, RIB * SWEEPS + s, :, 0:16] = costs[s * RIB : (s + 1) * RIB]

    def costs_ref(first_element):
        return winds[0, RIB * SWEEPS + first_element // RIB, :, 0:16]

    def results(t):
        at = pl.ds(t * 2 * RIB, 2 * RIB)
        return (
            pltpu.make_async_copy(dyn.at[at], dyn_hbm.at[at], out_sem.at[0, t]),
            pltpu.make_async_copy(phys.at[at], phys_hbm.at[at], out_sem.at[1, t]),
        )

    if opening:
        send_plan.wait()
        arrive(0)
        arrive(SWEEPS - 1)
        sub = sublanes()

        def edges(e, _):
            def low(t, v, value):
                if t == 0:
                    edge_low[e, :, 128 * v : 128 * (v + 1)] = jnp.where(
                        sub >= 4, turned(value, sub ^ 4), 0.0
                    )

            def high(t, v, value):
                edge_high[e, :, 128 * v : 128 * (v + 1)] = jnp.where(
                    sub < 4, turned(value, sub ^ 4), 0.0
                )

            advect(e, e + RIB, emit=low)
            advect(e + RIB * (SWEEPS - 1), e + RIB * SWEEPS, (1,), high)
            return 0

        lax.fori_loop(0, RIB, edges, 0, unroll=4)
        for copy in loads:
            copy.wait()
        wm[3] = (dot(wo[...], wi[...]) * 0.5).astype(BF16)
        wi[...] = wi[...] * 0.5
        for k in range(3):
            wm[k] = wm[k] * 0.5
    else:
        arrive(2 * first_step - 1)
        arrive(2 * first_step)

        def before(e, _):
            number = e + (2 * first_step - 1) * RIB
            advect(number, number + RIB)
            return 0

        lax.fori_loop(0, 2 * RIB, before, 0, unroll=4)

    def step(t, _):
        arrive(2 * t + 1)

        @pl.when(t < STEPS - 1)
        def _():
            arrive(2 * t + 2)

        def tasks():
            for e in range(32):
                number = t * 32 + RIB + e
                if e < RIB:
                    advect(number, number + RIB)
                else:
                    advect(
                        jnp.minimum(number, RIB * SWEEPS - RIB + e - RIB),
                        jnp.where(
                            t == STEPS - 1, RIB * (SWEEPS + 2) + e - RIB, number + RIB
                        ),
                    )
                    assemble(t * 32 + e - RIB)
                yield
            for e in range(RIB):
                assemble(t * 32 + RIB + e)
                yield

        chains = [
            network(t * 32 + c * RIB, column_counts(t * 32 + c * RIB)) for c in range(2)
        ]
        left = tasks()
        share = 0.0
        for _ in range(LAYERS):
            for chain in chains:
                pace = next(chain)
                state[RIB * SWEEPS, 0:8, 0:128] = pace
                adv[0, 16 * RIB * (SWEEPS + 3) :, :] = pace
                share += 48 / (2 * LAYERS)
                while share >= 1.0:
                    next(left)
                    share -= 1.0
        for rest in (*chains, left):
            for _ in rest:
                pass
        for copy in results(t):
            copy.start()
        return 0

    lax.fori_loop(first_step, last_step, step, 0)
    t = 0 if opening else 1
    part[...] = dyn[pl.ds(t * RIB * (SWEEPS - 1), RIB), 8 * t : 8 * t + 8, :]
    each(first_step, last_step, lambda s: [copy.wait() for copy in results(s)])


def halo_kernel(
    base, plan, table, before, after, part_low, part_high, dyn_in, dyn_hbm, low, high, sem
):
    last = RIB * (SWEEPS - 1)
    sub = sublanes()
    for near, part, t, halo, first in (
        (low, part_low, 0, before, 0),
        (high, part_high, 1, after, last),
    ):
        origin = RIB * (SWEEPS + 1) if t else 0
        slots = (0, 5, 4) if t else (1, 7, 6)
        left, right = 4 * t, 4 * t + 3

        def run(e, _):
            own = e + first
            at = [(plan[c, own] >> 4) - origin for c in slots]
            entry = plan[8 + t, own]
            for v in range(4):
                lanes = slice(128 * v, 128 * (v + 1))
                diagonal = jnp.where(
                    sub == left,
                    pltpu.roll(halo[at[1], :, lanes], 5, 0),
                    pltpu.roll(halo[at[2], :, lanes], 3, 0),
                )
                near[e, :, lanes] = (
                    part[e, :, lanes]
                    + halo[at[0], :, lanes] * table[entry]
                    + diagonal * table[entry + 1]
                )
            return 0

        lax.fori_loop(0, RIB, run, 0, unroll=8)
        pltpu.make_async_copy(
            near, dyn_hbm.at[pl.ds(first, RIB), pl.ds(8 * t, 8)], sem.at[t]
        ).start()
    for near, t, first in ((low, 0, 0), (high, 1, last)):
        pltpu.make_async_copy(
            near, dyn_hbm.at[pl.ds(first, RIB), pl.ds(8 * t, 8)], sem.at[t]
        ).wait()


def body(state, winds, neighbours, valence, cost, w_in, w_mid, w_out):
    vmem = pl.BlockSpec(memory_space=pltpu.VMEM)
    smem = pl.BlockSpec(memory_space=pltpu.SMEM)
    hbm = pl.BlockSpec(memory_space=pltpu.HBM)
    devices = lax.axis_size("dev")
    base = (lax.axis_index("dev") * (RIB * SWEEPS)).astype(jnp.int32).reshape(1)
    table = jnp.asarray(TABLE)
    dyn = jax.ShapeDtypeStruct(state.shape, F32)
    phys = jax.ShapeDtypeStruct(state.shape, BF16)
    edge = jax.ShapeDtypeStruct((RIB, 8, 512), F32)
    scratch = [
        pltpu.VMEM((RIB * SWEEPS + 1, 16, 512), F32),
        pltpu.VMEM((2, RIB * SWEEPS + SWEEPS, 16, 128), F32),
        pltpu.VMEM((4, (SWEEPS + 3) * RIB * 16 + 8, 128), F32),
        pltpu.VMEM((RIB * SWEEPS, 16, 512), F32),
        pltpu.VMEM((RIB * SWEEPS, 16, 512), BF16),
    ]
    semaphores = [pltpu.SemaphoreType.DMA((3, SWEEPS)), pltpu.SemaphoreType.DMA((2, STEPS))]
    params = dict(
        compiler_params=pltpu.CompilerParams(vmem_limit_bytes=40 * 2**20),
        cost_estimate=pl.CostEstimate(
            flops=6_000_000_000, bytes_accessed=7_000_000, transcendentals=5_000_000
        ),
    )
    costs = cost.T
    dyn, phys, low, high, part_low, plan, wi, wm, wo = pl.pallas_call(
        functools.partial(main_kernel, True),
        out_shape=(
            dyn,
            phys,
            edge,
            edge,
            edge,
            jax.ShapeDtypeStruct((16, RIB * SWEEPS), jnp.int32),
            jax.ShapeDtypeStruct(w_in.shape, BF16),
            jax.ShapeDtypeStruct((4, 384, 384), BF16),
            jax.ShapeDtypeStruct(w_out.shape, BF16),
        ),
        in_specs=[smem] + [vmem] * 4 + [hbm] * 5,
        out_specs=[hbm] * 2 + [vmem] * 7,
        scratch_shapes=scratch
        + [
            pltpu.SMEM((16, RIB * SWEEPS), jnp.int32),
            pltpu.SemaphoreType.DMA(()),
            pltpu.SemaphoreType.DMA((3,)),
        ]
        + semaphores,
        **params,
    )(base, neighbours.T, valence.T, costs, table, w_in, w_mid, w_out, state, winds)
    forward = [(i, (i + 1) % devices) for i in range(devices)]
    backward = [(target, source) for source, target in forward]
    before = lax.ppermute(high, "dev", forward)
    after = lax.ppermute(low, "dev", backward)

    dyn, phys, part_high = pl.pallas_call(
        functools.partial(main_kernel, False),
        out_shape=(
            jax.ShapeDtypeStruct(state.shape, F32),
            jax.ShapeDtypeStruct(state.shape, BF16),
            edge,
        ),
        in_specs=[smem] * 2 + [vmem] * 5 + [hbm] * 4,
        out_specs=[hbm] * 2 + [vmem],
        scratch_shapes=scratch + semaphores,
        input_output_aliases={9: 0, 10: 1},
        **params,
    )(base, plan, costs, table, wi, wm, wo, state, winds, dyn, phys)

    dyn = pl.pallas_call(
        halo_kernel,
        out_shape=jax.ShapeDtypeStruct(state.shape, F32),
        in_specs=[smem] * 2 + [vmem] * 5 + [hbm],
        out_specs=hbm,
        scratch_shapes=[
            pltpu.VMEM((RIB, 8, 512), F32),
            pltpu.VMEM((RIB, 8, 512), F32),
            pltpu.SemaphoreType.DMA((2,)),
        ],
        input_output_aliases={7: 0},
        cost_estimate=pl.CostEstimate(
            flops=1_000_000, bytes_accessed=2_000_000, transcendentals=0
        ),
    )(base, plan, table, before, after, part_low, part_high, dyn)
    return dyn, phys


def solution(mesh):
    return jax.shard_map(
        body,
        mesh=mesh,
        in_specs=(
            P("dev", None, None),
            P(None, "dev", None, None),
            P("dev", None),
            P("dev", None),
            P("dev", None),
            P(),
            P(),
            P(),
        ),
        out_specs=(P("dev", None, None), P("dev", None, None)),
        check_vma=False,
    )
```

time: 55.4 us -> 56.6 us (1.022)
  local copies, waits for them, and re-layouts: 5.91 us -> 12.1 us
  Pallas kernels: 40 us -> 34.9 us
    unnamed x27 -> x34, local copies, waits for them, and re-layouts: 5.91 us -> 12.1 us
    pallas_call x1, Pallas kernels: 5.1 us -> 2.23 us  [body(): pl.pallas_call(halo_kernel, out_shape=jax.ShapeDtypeStruct(state.shape, F...]
    pallas_call x2, Pallas kernels: 34.9 us -> 32.7 us  [the longest x1 17 us: body(): pl.pallas_call(functools.partial(main_kernel, True), out_shape=(dyn, phys...]
  transfers between devices with their start and end apart: 2 -> 2, of which waited for: 0 -> 0; matrix products, arithmetic and copies ran while one was open for 2% -> 0% of each run, Pallas kernels for 59% -> 28%
where the time goes in v1:
time: 56.6 us; the launch traced here: 56.1 us
  Pallas kernels  34.9 us (62%)
  local copies, waits for them, and re-layouts  12.1 us (21%)
  starting transfers between devices  8.25 us (15%)
  between operations  0.87 us (2%)
    pallas_call x1, Pallas kernels, body(): pl.pallas_call(functools.partial(main_kernel, True), out_shape=(dyn, phys...  17 us
    pallas_call x1, Pallas kernels, body(): pl.pallas_call(functools.partial(main_kernel, False), out_shape=(jax.Shap...  15.8 us
    unnamed x34, local copies, waits for them, and re-layouts  12.1 us
    ppermute x1, starting transfers between devices, body(): after = lax.ppermute(low, 'dev', backward)  8.25 us
    pallas_call x1, Pallas kernels, body(): pl.pallas_call(halo_kernel, out_shape=jax.ShapeDtypeStruct(state.shape, F...  2.23 us
  transfers between devices with their start and end apart: 2, of which 0 were waited for; matrix products, arithmetic and copies ran while one was open for 0% of the time, Pallas kernels for 28%

profile of v1, /device:TPU:0, one launch (start us, length us, event | category | flops | bytes accessed | tf_op | source)
XLA Modules:
  0.0 56.1 jit_solution(6783158516044102770)
XLA Ops:
  0.6 0.0 copy-start.2
  0.6 0.9 %copy-done.2 = f32[28,8,128]{2,1,0:T(8,128)S(1)} copy-done((f32[28,8,128]{2,1,0:T(8,128)S(1)}, f32[28,8,128]{2,1,0:T(8,128)}, u32[]{:S(2)}) %copy-start.2) | copy-done | bytes 114712
  1.5 0.0 copy-start.5
  1.5 2.2 %copy-done.5 = f32[128,16,512]{2,1,0:T(8,128)S(1)} copy-done((f32[128,16,512]{2,1,0:T(8,128)S(1)}, f32[128,16,512]{2,1,0:T(8,128)}, u32[]{:S(2)}) %copy-start.5) | copy-done | bytes 4194328
  3.7 0.0 copy-start.7
  3.7 1.6 %copy-done.7 = f32[2,128,16,128]{3,2,1,0:T(8,128)S(1)} copy-done((f32[2,128,16,128]{3,2,1,0:T(8,128)S(1)}, f32[2,128,16,128]{3,2,1,0:T(8,128)}, u32[]{:S(2)}) %copy-start.7) | copy-done | bytes 2097176
  5.3 0.0 copy-start.9
  5.3 1.2 %copy-done.9 = bf16[3,384,384]{2,1,0:T(8,128)(2,1)S(1)} copy-done((bf16[3,384,384]{2,1,0:T(8,128)(2,1)S(1)}, bf16[3,384,384]{2,1,0:T(8,128)(2,1)}, u32[]{:S(2)}) %copy-start.9) | copy-done | bytes 884760
  6.5 0.0 copy-start.10
  6.5 1.0 %copy-done.10 = bf16[512,384]{1,0:T(8,128)(2,1)S(1)} copy-done((bf16[512,384]{1,0:T(8,128)(2,1)S(1)}, bf16[512,384]{1,0:T(8,128)(2,1)}, u32[]{:S(2)}) %copy-start.10) | copy-done | bytes 393240
  7.5 1.0 %copy-done.11 = bf16[384,512]{1,0:T(8,128)(2,1)S(1)} copy-done((bf16[384,512]{1,0:T(8,128)(2,1)S(1)}, bf16[384,512]{1,0:T(8,128)(2,1)}, u32[]{:S(2)}) %copy-start.11) | copy-done | bytes 393240
  8.5 0.7 %copy-done.12 = s32[128,16]{0,1:T(8,128)S(1)} copy-done((s32[128,16]{0,1:T(8,128)S(1)}, s32[128,16]{0,1:T(8,128)}, u32[]{:S(2)}) %copy-start.12) | copy-done | bytes 8216
  9.2 0.7 %copy-done.13 = s32[128,8]{0,1:T(8,128)S(1)} copy-done((s32[128,8]{0,1:T(8,128)S(1)}, s32[128,8]{0,1:T(8,128)}, u32[]{:S(2)}) %copy-start.13) | copy-done | bytes 4120
  9.9 0.7 %copy-done.14 = s32[128,4]{0,1:T(4,128)S(1)} copy-done((s32[128,4]{0,1:T(4,128)S(1)}, s32[128,4]{0,1:T(4,128)}, u32[]{:S(2)}) %copy-start.14) | copy-done | bytes 2072
  10.6 17.0 %shard_map.104 = (f32[128,16,512]{2,1,0:T(8,128)}, bf16[128,16,512]{2,1,0:T(8,128)(2,1)}, f32[16,8,512]{2,1,0:T(8,128)S(1)}, f32[16,8,512]{2,1,0:T(8,128)S(1)}, ...) custom-call(s32[1]{0:T(128)} %bitcast.refs_0_.base, ...), custom_call_target="tpu_custom_call" | custom-call | flops 6000000000 | bytes 7000000 | tf_op jit(solution)/shard_map/pallas_call | solution.py:431
  27.5 0.0 copy-start
  27.5 0.7 %copy-done = f32[16,8,512]{2,1,0:T(8,128)} copy-done((f32[16,8,512]{2,1,0:T(8,128)}, f32[16,8,512]{2,1,0:T(8,128)S(1)}, u32[]{:S(2)}) %copy-start) | copy-done | bytes 262168
  28.2 0.0 collective-permute-start
  28.2 8.3 %collective-permute-start.1 = (f32[16,8,512]{2,1,0:T(8,128)S(1)}, f32[16,8,512]{2,1,0:T(8,128)S(1)}, u32[]{:S(2)}, u32[]{:S(2)}) collective-permute-start(f32[16,8,512]{2,1,0:T(8,128)S(1)} %get-tuple-element.16), channel_id=1, source_target_pairs={{1,0},{2,1},{3,2},{4,3},{5,4},{6,5},{7,6},{8,7},{9,8},{10,9},{11,1... | collective-permute-start | bytes 786440 | tf_op jit(solution)/shard_map/ppermute | solution.py:458
  36.5 0.0 copy-done.3
  36.5 0.0 copy-done.6
  36.5 0.0 copy-done.8
  36.5 15.8 %shard_map.105 = (f32[128,16,512]{2,1,0:T(8,128)}, bf16[128,16,512]{2,1,0:T(8,128)(2,1)}, f32[16,8,512]{2,1,0:T(8,128)S(1)}) custom-call(s32[1]{0:T(128)} %bitcast.refs_0_.base, s32[16,128]{1,0:T(8,128)S(1)} %get-tuple-element.14.refs_1_.plan, s32[16,128]{1,0:T(8,128)S(1)} %bitcast.5, ...), custom_call_target="tpu_custom_call", output_to_operand_aliasing={{0}: (9, {}), {1}: (10, {})} | custom-call | flops 6000000000 | bytes 7000000 | tf_op jit(solution)/shard_map/pallas_call | solution.py:460
  52.3 0.0 copy-done.4
  52.3 0.0 copy-start.1
  52.3 0.7 %copy-done.1 = f32[16,8,512]{2,1,0:T(8,128)} copy-done((f32[16,8,512]{2,1,0:T(8,128)}, f32[16,8,512]{2,1,0:T(8,128)S(1)}, u32[]{:S(2)}) %copy-start.1) | copy-done | bytes 262168
  53.0 0.0 collective-permute-done.before
  53.0 0.0 collective-permute-done.1.after
  53.0 0.0 copy-start.16
  53.0 0.7 %copy-done.15 = f32[16,8,512]{2,1,0:T(8,128)} copy-done((f32[16,8,512]{2,1,0:T(8,128)}, f32[16,8,512]{2,1,0:T(8,128)S(1)}, u32[]{:S(2)}) %copy-start.15) | copy-done | bytes 262168
  53.7 0.1 copy-done.16
  53.8 2.2 %shard_map.106 = f32[128,16,512]{2,1,0:T(8,128)} custom-call(s32[1]{0:T(128)} %bitcast.refs_0_.base, s32[16,128]{1,0:T(8,128)} %copy-done.4, f32[28,8,128]{2,1,0:T(8,128)} %constant.8.clone.refs_4_.refs_3_.table, f32[16,8,512]{2,1,0:T(8,128)} %copy-done.15, f32[16,8,512]{2,1,0:T(8,128)} %copy-done.16, ...), custom_call_target="tpu_custom_call", output_to_operand_aliasing={{}: (7, {})} | custom-call | flops 1000000 | bytes 2000000 | tf_op jit(solution)/shard_map/pallas_call | solution.py:474
  (9 shorter events, 0.0 us)
Async XLA Ops:
  0.6 0.9 %copy-start.2 = (f32[28,8,128]{2,1,0:T(8,128)S(1)}, f32[28,8,128]{2,1,0:T(8,128)}, u32[]{:S(2)}) copy-start(f32[28,8,128]{2,1,0:T(8,128)} %constant.8.clone.refs_4_.refs_3_.table) | copy-start | bytes 344068
  1.5 2.2 %copy-start.5 = (f32[128,16,512]{2,1,0:T(8,128)S(1)}, f32[128,16,512]{2,1,0:T(8,128)}, u32[]{:S(2)}) copy-start(f32[128,16,512]{2,1,0:T(8,128)} %refs_7_.3) | copy-start | bytes 12582916
  3.7 1.6 %copy-start.7 = (f32[2,128,16,128]{3,2,1,0:T(8,128)S(1)}, f32[2,128,16,128]{3,2,1,0:T(8,128)}, u32[]{:S(2)}) copy-start(f32[2,128,16,128]{3,2,1,0:T(8,128)} %refs_8_.3) | copy-start | bytes 6291460
  5.3 1.2 %copy-start.9 = (bf16[3,384,384]{2,1,0:T(8,128)(2,1)S(1)}, bf16[3,384,384]{2,1,0:T(8,128)(2,1)}, u32[]{:S(2)}) copy-start(bf16[3,384,384]{2,1,0:T(8,128)(2,1)} %refs_6_.1) | copy-start | bytes 2654212
  6.5 1.0 %copy-start.10 = (bf16[512,384]{1,0:T(8,128)(2,1)S(1)}, bf16[512,384]{1,0:T(8,128)(2,1)}, u32[]{:S(2)}) copy-start(bf16[512,384]{1,0:T(8,128)(2,1)} %refs_5_.1) | copy-start | bytes 1179652
  7.5 1.0 %copy-start.11 = (bf16[384,512]{1,0:T(8,128)(2,1)S(1)}, bf16[384,512]{1,0:T(8,128)(2,1)}, u32[]{:S(2)}) copy-start(bf16[384,512]{1,0:T(8,128)(2,1)} %refs_7_.2) | copy-start | bytes 1179652
  8.5 0.7 %copy-start.12 = (s32[128,16]{0,1:T(8,128)S(1)}, s32[128,16]{0,1:T(8,128)}, u32[]{:S(2)}) copy-start(s32[128,16]{0,1:T(8,128)} %param.13) | copy-start | bytes 24580
  9.2 0.7 %copy-start.13 = (s32[128,8]{0,1:T(8,128)S(1)}, s32[128,8]{0,1:T(8,128)}, u32[]{:S(2)}) copy-start(s32[128,8]{0,1:T(8,128)} %param.11) | copy-start | bytes 12292
  9.9 0.7 %copy-start.14 = (s32[128,4]{0,1:T(4,128)S(1)}, s32[128,4]{0,1:T(4,128)}, u32[]{:S(2)}) copy-start(s32[128,4]{0,1:T(4,128)} %param.12) | copy-start | bytes 6148
  10.5 25.9 %copy-start.3 = (f32[28,8,128]{2,1,0:T(8,128)S(1)}, f32[28,8,128]{2,1,0:T(8,128)}, u32[]{:S(2)}) copy-start(f32[28,8,128]{2,1,0:T(8,128)} %constant.8.clone.refs_4_.refs_3_.table) | copy-start | bytes 344068
  10.5 25.9 %copy-start.6 = (f32[128,16,512]{2,1,0:T(8,128)S(1)}, f32[128,16,512]{2,1,0:T(8,128)}, u32[]{:S(2)}) copy-start(f32[128,16,512]{2,1,0:T(8,128)} %refs_7_.3) | copy-start | bytes 12582916
  10.6 25.9 %copy-start.8 = (f32[2,128,16,128]{3,2,1,0:T(8,128)S(1)}, f32[2,128,16,128]{3,2,1,0:T(8,128)}, u32[]{:S(2)}) copy-start(f32[2,128,16,128]{3,2,1,0:T(8,128)} %refs_8_.3) | copy-start | bytes 6291460
  27.5 0.7 %copy-start = (f32[16,8,512]{2,1,0:T(8,128)}, f32[16,8,512]{2,1,0:T(8,128)S(1)}, u32[]{:S(2)}) copy-start(f32[16,8,512]{2,1,0:T(8,128)S(1)} %get-tuple-element.17.part_low) | copy-start | bytes 786436
  28.2 24.0 %copy-start.4 = (s32[16,128]{1,0:T(8,128)}, s32[16,128]{1,0:T(8,128)S(1)}, u32[]{:S(2)}) copy-start(s32[16,128]{1,0:T(8,128)S(1)} %get-tuple-element.14.refs_1_.plan) | copy-start | bytes 24580
  28.2 24.7 %collective-permute-start = (f32[16,8,512]{2,1,0:T(8,128)S(1)}, f32[16,8,512]{2,1,0:T(8,128)S(1)}, u32[]{:S(2)}, u32[]{:S(2)}) collective-permute-start(f32[16,8,512]{2,1,0:T(8,128)S(1)} %get-tuple-element.15), channel_id=1, source_target_pairs={{0,1},{1,2},{2,3},{3,4},{4,5},{5,6},{6,7},{7,8},{8,9},{9,10},{10,1... | collective-permute-start | bytes 786440 | tf_op jit(solution)/shard_map/ppermute | solution.py:457
  28.2 24.7 %collective-permute-start.1 = (f32[16,8,512]{2,1,0:T(8,128)S(1)}, f32[16,8,512]{2,1,0:T(8,128)S(1)}, u32[]{:S(2)}, u32[]{:S(2)}) collective-permute-start(f32[16,8,512]{2,1,0:T(8,128)S(1)} %get-tuple-element.16), channel_id=1, source_target_pairs={{1,0},{2,1},{3,2},{4,3},{5,4},{6,5},{7,6},{8,7},{9,8},{10,9},{11,1... | collective-permute-start | bytes 786440 | tf_op jit(solution)/shard_map/ppermute | solution.py:458
  52.3 0.7 %copy-start.1 = (f32[16,8,512]{2,1,0:T(8,128)}, f32[16,8,512]{2,1,0:T(8,128)S(1)}, u32[]{:S(2)}) copy-start(f32[16,8,512]{2,1,0:T(8,128)S(1)} %get-tuple-element.23.part_high) | copy-start | bytes 786436
  53.0 0.7 %copy-start.15 = (f32[16,8,512]{2,1,0:T(8,128)}, f32[16,8,512]{2,1,0:T(8,128)S(1)}, u32[]{:S(2)}) copy-start(f32[16,8,512]{2,1,0:T(8,128)S(1)} %collective-permute-done.before) | copy-start | bytes 786436
  53.0 0.8 %copy-start.16 = (f32[16,8,512]{2,1,0:T(8,128)}, f32[16,8,512]{2,1,0:T(8,128)S(1)}, u32[]{:S(2)}) copy-start(f32[16,8,512]{2,1,0:T(8,128)S(1)} %collective-permute-done.1.after) | copy-start | bytes 786436

commit v2 on v1

v2 whole, which is shorter than its diff:
```python
import functools

import jax
import jax.numpy as jnp
import numpy as np
from jax import lax
from jax.experimental import pallas as pl
from jax.experimental.pallas import tpu as pltpu
from jax.sharding import PartitionSpec as P

RIB = 16
SUB = 4
SWEEPS = 8
STEPS = 4
ALL = 16384
F32 = jnp.float32
BF16 = jnp.bfloat16


def lobatto_table():
    nodes = np.array([-1.0, -1.0 / np.sqrt(5.0), 1.0 / np.sqrt(5.0), 1.0])
    weights = np.array(
        [
            1.0 / np.prod([nodes[outer] - nodes[inner] for inner in range(4) if inner != outer])
            for outer in range(4)
        ]
    )
    deriv = np.zeros((4, 4))
    for outer in range(4):
        for inner in range(4):
            if inner != outer:
                deriv[outer, inner] = weights[inner] / weights[outer] / (nodes[outer] - nodes[inner])
        deriv[outer, outer] = -np.sum(deriv[outer])
    return deriv.astype(np.float32)


def constant_table():
    deriv = lobatto_table()
    sub = np.arange(8)
    half, along = sub // 4, sub % 4
    rows = []
    for t in range(2):
        i = 2 * t + half
        for source in (half, 1 - half, 2 + half, 3 - half):
            rows.append(-deriv[i, source])
    for shift in range(4):
        rows.append(-deriv[along, (along + shift) % 4])
    for t in range(2):
        first, second = (0, 3) if t == 0 else (4, 7)
        edge = np.ones(8)
        edge += (half == t) * 1.0
        edge += (along == 0) * 1.0
        edge += (along == 3) * 1.0
        for pattern in range(4):
            present = np.zeros(8)
            present[first] = pattern // 2
            present[second] = pattern % 2
            rows.append(1.0 / (edge + present))
            rows.append(present / (edge + present))
    table = np.stack(rows).astype(np.float32)
    return np.ascontiguousarray(np.broadcast_to(table[:, :, None], table.shape + (128,)))


TABLE = constant_table()
A_AT, B_AT, W_AT = 0, 8, 12


def dot(a, b):
    return jnp.dot(a, b, preferred_element_type=F32)


def silu_half(h):
    h = h.astype(BF16)
    return h + h * jnp.tanh(h)


def sublanes():
    return lax.broadcasted_iota(jnp.int32, (8, 128), 0)


def turned(tile, pattern):
    return jnp.take_along_axis(tile, pattern, axis=0, mode="promise_in_bounds")


def element_advect(load, wind, table, halves, emit):
    sub = sublanes()
    swap = sub ^ 4
    shifts = [(sub & 4) | ((sub + shift) & 3) for shift in range(4)]
    for v in range(4):
        low, high = load(0, v), load(1, v)
        pieces = (low, turned(low, swap), high, turned(high, swap))
        for t in halves:
            own = (low, high)[t]
            da = pieces[0] * table[A_AT + 4 * t]
            for k in range(1, 4):
                da = da + pieces[k] * table[A_AT + 4 * t + k]
            db = own * table[B_AT]
            for shift in range(1, 4):
                db = db + turned(own, shifts[shift]) * table[B_AT + shift]
            emit(t, v, wind(0, t) * da + wind(1, t) * db)


def main_kernel(
    base,
    neighbours,
    valence,
    cost,
    table,
    w_in,
    w_mid,
    w_out,
    state_hbm,
    winds_hbm,
    dyn_hbm,
    phys_hbm,
    low_hbm,
    high_hbm,
    state,
    winds,
    adv,
    dyn,
    phys,
    wi,
    wm,
    wo,
    edge_sum,
    edge_rows,
    edge_sent,
    plan_vmem,
    plan,
    most,
    plan_sem,
    w_sem,
    edge_sem,
    in_sem,
    out_sem,
):
    def copies(s):
        at = pl.ds(s * RIB, RIB)
        return (
            pltpu.make_async_copy(state_hbm.at[at], state.at[at], in_sem.at[0, s]),
            pltpu.make_async_copy(winds_hbm.at[0, at], winds.at[0, at], in_sem.at[1, s]),
            pltpu.make_async_copy(winds_hbm.at[1, at], winds.at[1, at], in_sem.at[2, s]),
        )

    def fetch(s):
        for copy in copies(s):
            copy.start()

    def arrive(s):
        for copy in copies(s):
            copy.wait()

    fetch(0)
    fetch(SWEEPS - 1)
    loads = [
        pltpu.make_async_copy(w_in, wi, w_sem.at[0]),
        pltpu.make_async_copy(w_mid, wm.at[pl.ds(0, 3)], w_sem.at[1]),
        pltpu.make_async_copy(w_out, wo, w_sem.at[2]),
    ]
    for copy in loads:
        copy.start()
    for s in range(1, SWEEPS - 1):
        fetch(s)
    plan_vmem[0:8, :] = ((neighbours[...] - base[0] + RIB) & (ALL - 1)) * 16
    corner = valence[...] - 3
    plan_vmem[8:9, :] = corner[3:4] * 4 + corner[2:3] * 2 + W_AT
    plan_vmem[9:10, :] = corner[1:2] * 4 + corner[0:1] * 2 + W_AT + 8
    plan_vmem[10:16, :] = jnp.zeros((6, 128), jnp.int32)
    send_plan = pltpu.make_async_copy(plan_vmem, plan, plan_sem)
    send_plan.start()
    edge_sum[...] = jnp.zeros(edge_sum.shape, F32)

    for v in range(4):
        adv[v, : 16 * RIB, :] = jnp.zeros((16 * RIB, 128), F32)
        adv[v, 16 * RIB * (SWEEPS + 1) : 16 * RIB * (SWEEPS + 2), :] = jnp.zeros(
            (16 * RIB, 128), F32
        )
    costs = lax.dot_general(
        cost[...].astype(BF16),
        (
            lax.broadcasted_iota(jnp.int32, (16, 16), 0)
            == lax.broadcasted_iota(jnp.int32, (16, 16), 1)
        ).astype(BF16),
        (((0,), (0,)), ((), ())),
        preferred_element_type=F32,
    )

    def advect(e, to, halves=(0, 1), emit=None):
        def keep(t, v, value):
            adv[v, pl.ds(pl.multiple_of(to * 16 + 8 * t, 8), 8), :] = value
            if emit is not None:
                emit(t, v, value)

        element_advect(
            lambda t, v: state[e, 8 * t : 8 * t + 8, 128 * v : 128 * (v + 1)],
            lambda d, t: winds[d, e, 8 * t : 8 * t + 8, :],
            table,
            halves,
            keep,
        )

    def assemble(e):
        sub = sublanes()
        along = sub % 4
        at = [plan[c, e] for c in range(8)]
        own_at = pl.multiple_of((e + RIB) * 16, 16)
        for t in range(2):
            entry = plan[8 + t, e]
            weight = table[entry]
            corner = table[entry + 1]
            for v in range(4):

                def rows(start):
                    return adv[v, pl.ds(start, 8), :]

                if t == 0:
                    across = jnp.where(sub < 4, rows(at[1] + 12), 0.0)
                    diagonal = jnp.where(sub == 0, rows(at[7] + 15), rows(at[6] + 9))
                else:
                    across = jnp.where(sub >= 4, rows(at[0] - 4), 0.0)
                    diagonal = jnp.where(sub == 4, rows(at[5] - 1), rows(at[4] - 7))
                beside = jnp.where(
                    along == 3,
                    rows(at[2] + 8 * t - 3),
                    jnp.where(along == 0, rows(at[3] + 8 * t + 3), 0.0),
                )
                own = adv[v, pl.ds(own_at + 8 * t, 8), :]
                dyn[e, 8 * t : 8 * t + 8, 128 * v : 128 * (v + 1)] = (
                    own + across + beside
                ) * weight + diagonal * corner

    def network(first_element, counts, substeps):
        x = state[pl.ds(first_element, RIB)].reshape(16 * RIB, 512).astype(BF16)
        a = dot(x, wi[...])
        yield a[:8, :128]
        total = None
        for s in range(substeps):
            h = silu_half(a)
            for k in range(3):
                pre = dot(h, wm[k])
                yield pre[:8, :128]
                h = silu_half(pre)
            wide = h.astype(F32)
            if s == 0:
                total = wide
            else:
                active = counts > s
                total = total + jnp.concatenate(
                    [
                        jnp.where(active, wide[:, 128 * v : 128 * (v + 1)], 0.0)
                        for v in range(3)
                    ],
                    1,
                )
            if s < substeps - 1:
                a = a + dot(h, wm[3])
                yield a[:8, :128]
        tend = dot(total.astype(BF16), wo[...])
        phys[pl.ds(first_element, RIB)] = tend.astype(BF16).reshape(RIB, 16, 512)

    for t in range(STEPS):
        most[t] = jnp.max(cost[:, 32 * t : 32 * t + 32])

    def column_counts(first_element):
        block = costs_ref(first_element)
        spread = jnp.broadcast_to(block[:, None, :], (RIB, 16, 16))
        point = lax.broadcasted_iota(jnp.int32, (RIB, 16, 16), 1)
        lane = lax.broadcasted_iota(jnp.int32, (RIB, 16, 16), 2)
        spread = jnp.where(point == lane, spread, 0.0).reshape(16 * RIB, 16)
        return dot(spread.astype(BF16), jnp.ones((16, 128), BF16))

    for s in range(SWEEPS):
        winds[0, RIB * SWEEPS + s, :, 0:16] = costs[s * RIB : (s + 1) * RIB]

    def costs_ref(first_element):
        return winds[0, RIB * SWEEPS + first_element // RIB, :, 0:16]

    def results(t):
        at = pl.ds(t * 2 * RIB, 2 * RIB)
        return (
            pltpu.make_async_copy(dyn.at[at], dyn_hbm.at[at], out_sem.at[0, t]),
            pltpu.make_async_copy(phys.at[at], phys_hbm.at[at], out_sem.at[1, t]),
        )

    send_plan.wait()
    arrive(0)
    arrive(SWEEPS - 1)
    sub = sublanes()
    swap = sub ^ 4

    def contribute(k, e):
        slots = (0, 5, 4) if k else (1, 7, 6)
        origin = RIB * (SWEEPS + 1) if k else 0
        at = [(plan[c, e] >> 4) - origin for c in slots]
        entry = plan[8 + k, e]
        weight, corner = table[entry], table[entry + 1]
        own = 4 * k
        far = 4 - own

        def emit(t, v, value):
            if t != k:
                return
            lanes = slice(128 * v, 128 * (v + 1))
            edge = turned(value * weight, swap)
            edge_sum[k, at[0], :, lanes] += jnp.where((sub >= far) & (sub < far + 4), edge, 0.0)
            diagonal = value * corner
            edge_sum[k, at[1], :, lanes] += jnp.where(
                sub == far + 3, pltpu.roll(diagonal, (far + 3 - own) % 8, 0), 0.0
            )
            edge_sum[k, at[2], :, lanes] += jnp.where(
                sub == far, pltpu.roll(diagonal, (far - own - 3) % 8, 0), 0.0
            )

        return emit

    def edges(e, _):
        advect(e, e + RIB, emit=contribute(0, e))
        last = e + RIB * (SWEEPS - 1)
        advect(last, last + RIB, (1,), contribute(1, last))
        return 0

    lax.fori_loop(0, RIB, edges, 0, unroll=4)
    for m in range(RIB // 2):
        for v in range(4):
            lanes = slice(128 * v, 128 * (v + 1))
            for k in range(2):
                first, second = edge_sum[k, 2 * m, :, lanes], edge_sum[k, 2 * m + 1, :, lanes]
                first, second = (first, turned(second, swap)) if k else (turned(first, swap), second)
                edge_rows[k, 8 * m : 8 * m + 8, lanes] = jnp.where(sub < 4, first, second)
    edge_sent[...] = edge_rows[...].astype(BF16)
    sent = [
        pltpu.make_async_copy(edge_sent.at[0], low_hbm, edge_sem.at[0]),
        pltpu.make_async_copy(edge_sent.at[1], high_hbm, edge_sem.at[1]),
    ]
    for copy in sent:
        copy.start()
    for copy in loads:
        copy.wait()
    wm[3] = (dot(wo[...], wi[...]) * 0.5).astype(BF16)
    wi[...] = wi[...] * 0.5
    for k in range(3):
        wm[k] = wm[k] * 0.5

    def step(t, _):
        @pl.when(t < STEPS - 1)
        def _():
            arrive(2 * t + 1)
            arrive(2 * t + 2)

        def tasks():
            for e in range(32):
                number = t * 32 + RIB + e
                if e < RIB:
                    advect(number, number + RIB)
                else:
                    advect(
                        jnp.minimum(number, RIB * SWEEPS - RIB + e - RIB),
                        jnp.where(
                            t == STEPS - 1, RIB * (SWEEPS + 2) + e - RIB, number + RIB
                        ),
                    )
                    assemble(t * 32 + e - RIB)
                yield
            for e in range(RIB):
                assemble(t * 32 + RIB + e)
                yield

        def work(substeps):
            chains = [
                network(t * 32 + c * RIB, column_counts(t * 32 + c * RIB), substeps)
                for c in range(2)
            ]
            left = tasks()
            layers = 4 * substeps
            share = 0.0
            for _ in range(layers):
                for chain in chains:
                    pace = next(chain)
                    state[RIB * SWEEPS, 0:8, 0:128] = pace
                    adv[0, 16 * RIB * (SWEEPS + 3) :, :] = pace
                    share += 48 / (2 * layers)
                    while share >= 1.0:
                        next(left)
                        share -= 1.0
            for rest in (*chains, left):
                for _ in rest:
                    pass

        for substeps in range(1, SUB + 1):
            pl.when(most[t] == substeps)(functools.partial(work, substeps))
        for copy in results(t):
            copy.start()
        return 0

    lax.fori_loop(0, STEPS, step, 0)
    for copy in sent:
        copy.wait()
    for t in range(STEPS):
        for copy in results(t):
            copy.wait()


def halo_kernel(before_hbm, after_hbm, dyn_in, dyn_hbm, low, high, before, after, sem):
    last = RIB * (SWEEPS - 1)
    sub = sublanes()
    places = (
        (low, dyn_hbm.at[pl.ds(0, RIB), pl.ds(0, 8)]),
        (high, dyn_hbm.at[pl.ds(last, RIB), pl.ds(8, 8)]),
    )
    loads = [pltpu.make_async_copy(far, near, sem.at[k]) for k, (near, far) in enumerate(places)]
    stores = [
        pltpu.make_async_copy(near, far, sem.at[2 + k]) for k, (near, far) in enumerate(places)
    ]
    arrivals = [
        pltpu.make_async_copy(before_hbm, before, sem.at[4]),
        pltpu.make_async_copy(after_hbm, after, sem.at[5]),
    ]
    for copy in loads + arrivals:
        copy.start()
    for k, (near, halo) in enumerate(((low, before), (high, after))):
        loads[k].wait()
        arrivals[k].wait()
        kept = sub >= 4 if k else sub < 4
        for q in range(RIB // 4):
            packed = halo[16 * q : 16 * q + 16, :].astype(F32)
            for r in range(4):
                for v in range(4):
                    lanes = slice(128 * v, 128 * (v + 1))
                    tile = packed[8 * (r // 2) : 8 * (r // 2) + 8, lanes]
                    if r % 2 != k:
                        tile = pltpu.roll(tile, 4, 0)
                    near[4 * q + r, :, lanes] += jnp.where(kept, tile, 0.0)
        stores[k].start()
    for copy in stores:
        copy.wait()


def body(state, winds, neighbours, valence, cost, w_in, w_mid, w_out):
    vmem = pl.BlockSpec(memory_space=pltpu.VMEM)
    smem = pl.BlockSpec(memory_space=pltpu.SMEM)
    hbm = pl.BlockSpec(memory_space=pltpu.HBM)
    devices = lax.axis_size("dev")
    base = (lax.axis_index("dev") * (RIB * SWEEPS)).astype(jnp.int32).reshape(1)
    table = jnp.asarray(TABLE)
    edge = jax.ShapeDtypeStruct((RIB * 4, 512), BF16)
    dyn, phys, low, high = pl.pallas_call(
        main_kernel,
        out_shape=(
            jax.ShapeDtypeStruct(state.shape, F32),
            jax.ShapeDtypeStruct(state.shape, BF16),
            edge,
            edge,
        ),
        in_specs=[smem] + [vmem] * 4 + [hbm] * 5,
        out_specs=[hbm] * 4,
        scratch_shapes=[
            pltpu.VMEM((RIB * SWEEPS + 1, 16, 512), F32),
            pltpu.VMEM((2, RIB * SWEEPS + SWEEPS, 16, 128), F32),
            pltpu.VMEM((4, (SWEEPS + 3) * RIB * 16 + 8, 128), F32),
            pltpu.VMEM((RIB * SWEEPS, 16, 512), F32),
            pltpu.VMEM((RIB * SWEEPS, 16, 512), BF16),
            pltpu.VMEM(w_in.shape, BF16),
            pltpu.VMEM((4, 384, 384), BF16),
            pltpu.VMEM(w_out.shape, BF16),
            pltpu.VMEM((2, RIB, 8, 512), F32),
            pltpu.VMEM((2, RIB * 4, 512), F32),
            pltpu.VMEM((2, RIB * 4, 512), BF16),
            pltpu.VMEM((16, RIB * SWEEPS), jnp.int32),
            pltpu.SMEM((16, RIB * SWEEPS), jnp.int32),
            pltpu.SMEM((STEPS,), jnp.int32),
            pltpu.SemaphoreType.DMA(()),
            pltpu.SemaphoreType.DMA((3,)),
            pltpu.SemaphoreType.DMA((2,)),
            pltpu.SemaphoreType.DMA((3, SWEEPS)),
            pltpu.SemaphoreType.DMA((2, STEPS)),
        ],
        compiler_params=pltpu.CompilerParams(vmem_limit_bytes=63 * 2**20),
        cost_estimate=pl.CostEstimate(
            flops=12_000_000_000, bytes_accessed=14_000_000, transcendentals=10_000_000
        ),
    )(base, neighbours.T, valence.T, cost.T, table, w_in, w_mid, w_out, state, winds)
    forward = [(i, (i + 1) % devices) for i in range(devices)]
    backward = [(target, source) for source, target in forward]
    before = lax.ppermute(high, "dev", forward)
    after = lax.ppermute(low, "dev", backward)
    dyn = pl.pallas_call(
        halo_kernel,
        out_shape=jax.ShapeDtypeStruct(state.shape, F32),
        in_specs=[hbm] * 3,
        out_specs=hbm,
        scratch_shapes=[
            pltpu.VMEM((RIB, 8, 512), F32),
            pltpu.VMEM((RIB, 8, 512), F32),
            pltpu.VMEM((RIB * 4, 512), BF16),
            pltpu.VMEM((RIB * 4, 512), BF16),
            pltpu.SemaphoreType.DMA((6,)),
        ],
        input_output_aliases={2: 0},
        compiler_params=pltpu.CompilerParams(vmem_limit_bytes=63 * 2**20),
        cost_estimate=pl.CostEstimate(
            flops=1_000_000, bytes_accessed=2_000_000, transcendentals=0
        ),
    )(before, after, dyn)
    return dyn, phys


def solution(mesh):
    return jax.shard_map(
        body,
        mesh=mesh,
        in_specs=(
            P("dev", None, None),
            P(None, "dev", None, None),
            P("dev", None),
            P("dev", None),
            P("dev", None),
            P(),
            P(),
            P(),
        ),
        out_specs=(P("dev", None, None), P("dev", None, None)),
        check_vma=False,
    )
```

time: 56.6 us -> 40.5 us (0.72); the launches traced: 56.1 us -> 40.9 us
  local copies, waits for them, and re-layouts: 12.1 us -> 0.62 us
  Pallas kernels: 34.9 us -> 29 us
  waiting for transfers between devices: 0.01 us -> 2.22 us
    unnamed x34 -> x4, local copies, waits for them, and re-layouts: 12.1 us -> 0.62 us
    pallas_call x2 -> x1, Pallas kernels: 32.7 us -> 27.1 us  [body(): pl.pallas_call(main_kernel, out_shape=(jax.ShapeDtypeStruct(state.shape,...]
    ppermute x1, waiting for transfers between devices: 0.01 us -> 2.08 us  [body(): before = lax.ppermute(high, 'dev', forward)]
  transfers between devices with their start and end apart: 2 -> 2, of which waited for: 0 -> 2; matrix products, arithmetic and copies ran while one was open for 0% -> 0% of each run, Pallas kernels for 28% -> 0%
where the time goes in v2:
time: 40.5 us; the launch traced here: 40.9 us
  Pallas kernels  29 us (72%)
  starting transfers between devices  8.4 us (21%)
  waiting for transfers between devices  2.22 us (5%)
  between operations  0.66 us (2%)
  local copies, waits for them, and re-layouts  0.62 us (2%)
    pallas_call x1, Pallas kernels, body(): pl.pallas_call(main_kernel, out_shape=(jax.ShapeDtypeStruct(state.shape,...  27.1 us
    ppermute x1, starting transfers between devices, body(): after = lax.ppermute(low, 'dev', backward)  8.32 us
    ppermute x1, waiting for transfers between devices, body(): before = lax.ppermute(high, 'dev', forward)  2.08 us
    pallas_call x1, Pallas kernels, body(): pl.pallas_call(halo_kernel, out_shape=jax.ShapeDtypeStruct(state.shape, F...  1.86 us
  transfers between devices with their start and end apart: 2, of which 2 were waited for; matrix products, arithmetic and copies ran while one was open for 0% of the time, Pallas kernels for 0%

profile of v2, /device:TPU:0, one launch (start us, length us, event | category | flops | bytes accessed | tf_op | source)
XLA Modules:
  0.0 40.9 jit_solution(7861050884185114844)
XLA Ops:
  0.6 27.1 %shard_map.104 = (f32[128,16,512]{2,1,0:T(8,128)}, bf16[128,16,512]{2,1,0:T(8,128)(2,1)}, bf16[64,512]{1,0:T(8,128)(2,1)}, bf16[64,512]{1,0:T(8,128)(2,1)}) custom-call(s32[1]{0:T(128)} %bitcast.base, s32[8,128]{1,0:T(8,128)} %bitcast.5, s32[4,128]{1,0:T(4,128)} %bitcast.6, s32[16,128]{1,0:T(8,128)} %bitcast.4, f32[28,8,128]{2,1,0:T(8,128)} %constant.8.clone.table, ...), custom_call_target="tpu_custom_call" | custom-call | flops 12000000000 | bytes 14000000 | tf_op jit(solution)/shard_map/pallas_call | solution.py:447
  27.8 0.1 collective-permute-start
  27.8 8.3 %collective-permute-start.1 = (bf16[64,512]{1,0:T(8,128)(2,1)}, bf16[64,512]{1,0:T(8,128)(2,1)S(1)}, u32[]{:S(2)}, u32[]{:S(2)}) collective-permute-start(bf16[64,512]{1,0:T(8,128)(2,1)} %get-tuple-element.7), channel_id=1, source_target_pairs={{1,0},{2,1},{3,2},{4,3},{5,4},{6,5},{7,6},{8,7},{9,8},{10,9},{11,1... | collective-permute-start | bytes 196616 | tf_op jit(solution)/shard_map/ppermute | solution.py:486
  36.2 2.1 %collective-permute-done.before_hbm = bf16[64,512]{1,0:T(8,128)(2,1)S(1)} collective-permute-done((bf16[64,512]{1,0:T(8,128)(2,1)}, bf16[64,512]{1,0:T(8,128)(2,1)S(1)}, u32[]{:S(2)}, u32[]{:S(2)}) %collective-permute-start) | collective-permute-done | bytes 65568 | tf_op jit(solution)/shard_map/ppermute | solution.py:485
  38.2 0.0 copy-start
  38.2 0.1 collective-permute-done.1.after_hbm
  38.4 0.0 copy-start.1
  38.4 0.5 %copy-done = bf16[64,512]{1,0:T(8,128)(2,1)} copy-done((bf16[64,512]{1,0:T(8,128)(2,1)}, bf16[64,512]{1,0:T(8,128)(2,1)S(1)}, u32[]{:S(2)}) %copy-start) | copy-done | bytes 65560
  38.9 0.1 copy-done.1
  39.0 1.9 %shard_map.105 = f32[128,16,512]{2,1,0:T(8,128)} custom-call(bf16[64,512]{1,0:T(8,128)(2,1)} %copy-done, bf16[64,512]{1,0:T(8,128)(2,1)} %copy-done.1, f32[128,16,512]{2,1,0:T(8,128)} %get-tuple-element.8.dyn_in), custom_call_target="tpu_custom_call", output_to_operand_aliasing={{}: (2, {})} | custom-call | flops 1000000 | bytes 2000000 | tf_op jit(solution)/shard_map/pallas_call | solution.py:487
Async XLA Ops:
  27.8 10.5 %collective-permute-start = (bf16[64,512]{1,0:T(8,128)(2,1)}, bf16[64,512]{1,0:T(8,128)(2,1)S(1)}, u32[]{:S(2)}, u32[]{:S(2)}) collective-permute-start(bf16[64,512]{1,0:T(8,128)(2,1)} %get-tuple-element.6), channel_id=1, source_target_pairs={{0,1},{1,2},{2,3},{3,4},{4,5},{5,6},{6,7},{7,8},{8,9},{9,10},{10,1... | collective-permute-start | bytes 196616 | tf_op jit(solution)/shard_map/ppermute | solution.py:485
  27.8 10.5 %collective-permute-start.1 = (bf16[64,512]{1,0:T(8,128)(2,1)}, bf16[64,512]{1,0:T(8,128)(2,1)S(1)}, u32[]{:S(2)}, u32[]{:S(2)}) collective-permute-start(bf16[64,512]{1,0:T(8,128)(2,1)} %get-tuple-element.7), channel_id=1, source_target_pairs={{1,0},{2,1},{3,2},{4,3},{5,4},{6,5},{7,6},{8,7},{9,8},{10,9},{11,1... | collective-permute-start | bytes 196616 | tf_op jit(solution)/shard_map/ppermute | solution.py:486
  38.2 0.6 %copy-start = (bf16[64,512]{1,0:T(8,128)(2,1)}, bf16[64,512]{1,0:T(8,128)(2,1)S(1)}, u32[]{:S(2)}) copy-start(bf16[64,512]{1,0:T(8,128)(2,1)S(1)} %collective-permute-done.before_hbm) | copy-start | bytes 196612
  38.4 0.6 %copy-start.1 = (bf16[64,512]{1,0:T(8,128)(2,1)}, bf16[64,512]{1,0:T(8,128)(2,1)S(1)}, u32[]{:S(2)}) copy-start(bf16[64,512]{1,0:T(8,128)(2,1)S(1)} %collective-permute-done.1.after_hbm) | copy-start | bytes 196612

commit v3 on v2

--- a/solution.py
+++ b/solution.py
@@ -102,10 +102,10 @@
 
 def main_kernel(
     base,
-    neighbours,
-    valence,
-    cost,
-    table,
+    neighbours_hbm,
+    valence_hbm,
+    cost_hbm,
+    table_hbm,
     w_in,
     w_mid,
     w_out,
@@ -115,6 +115,10 @@
     phys_hbm,
     low_hbm,
     high_hbm,
+    neighbours,
+    valence,
+    cost,
+    table,
     state,
     winds,
     adv,
@@ -130,6 +134,7 @@
     plan,
     most,
     plan_sem,
+    small_sem,
     w_sem,
     edge_sem,
     in_sem,
@@ -151,6 +156,14 @@
         for copy in copies(s):
             copy.wait()
 
+    small = [
+        pltpu.make_async_copy(neighbours_hbm, neighbours, small_sem.at[0]),
+        pltpu.make_async_copy(valence_hbm, valence, small_sem.at[1]),
+        pltpu.make_async_copy(table_hbm, table, small_sem.at[2]),
+        pltpu.make_async_copy(cost_hbm, cost, small_sem.at[3]),
+    ]
+    for copy in small:
+        copy.start()
     fetch(0)
     fetch(SWEEPS - 1)
     loads = [
@@ -162,6 +175,13 @@
         copy.start()
     for s in range(1, SWEEPS - 1):
         fetch(s)
+    for v in range(4):
+        adv[v, : 16 * RIB, :] = jnp.zeros((16 * RIB, 128), F32)
+        adv[v, 16 * RIB * (SWEEPS + 1) : 16 * RIB * (SWEEPS + 2), :] = jnp.zeros(
+            (16 * RIB, 128), F32
+        )
+    for copy in small:
+        copy.wait()
     plan_vmem[0:8, :] = ((neighbours[...] - base[0] + RIB) & (ALL - 1)) * 16
     corner = valence[...] - 3
     plan_vmem[8:9, :] = corner[3:4] * 4 + corner[2:3] * 2 + W_AT
@@ -169,13 +189,6 @@
     plan_vmem[10:16, :] = jnp.zeros((6, 128), jnp.int32)
     send_plan = pltpu.make_async_copy(plan_vmem, plan, plan_sem)
     send_plan.start()
-    edge_sum[...] = jnp.zeros(edge_sum.shape, F32)
-
-    for v in range(4):
-        adv[v, : 16 * RIB, :] = jnp.zeros((16 * RIB, 128), F32)
-        adv[v, 16 * RIB * (SWEEPS + 1) : 16 * RIB * (SWEEPS + 2), :] = jnp.zeros(
-            (16 * RIB, 128), F32
-        )
     costs = lax.dot_general(
         cost[...].astype(BF16),
         (
@@ -303,14 +316,10 @@
                 return
             lanes = slice(128 * v, 128 * (v + 1))
             edge = turned(value * weight, swap)
-            edge_sum[k, at[0], :, lanes] += jnp.where((sub >= far) & (sub < far + 4), edge, 0.0)
+            edge_sum[k, 0, at[0], :, lanes] = edge
             diagonal = value * corner
-            edge_sum[k, at[1], :, lanes] += jnp.where(
-                sub == far + 3, pltpu.roll(diagonal, (far + 3 - own) % 8, 0), 0.0
-            )
-            edge_sum[k, at[2], :, lanes] += jnp.where(
-                sub == far, pltpu.roll(diagonal, (far - own - 3) % 8, 0), 0.0
-            )
+            edge_sum[k, 1, at[1], :, lanes] = pltpu.roll(diagonal, (far + 3 - own) % 8, 0)
+            edge_sum[k, 2, at[2], :, lanes] = pltpu.roll(diagonal, (far - own - 3) % 8, 0)
 
         return emit
 
@@ -325,7 +334,13 @@
         for v in range(4):
             lanes = slice(128 * v, 128 * (v + 1))
             for k in range(2):
-                first, second = edge_sum[k, 2 * m, :, lanes], edge_sum[k, 2 * m + 1, :, lanes]
+                far = 0 if k else 4
+                first, second = [
+                    edge_sum[k, 0, e, :, lanes]
+                    + jnp.where(sub == far + 3, edge_sum[k, 1, e, :, lanes], 0.0)
+                    + jnp.where(sub == far, edge_sum[k, 2, e, :, lanes], 0.0)
+                    for e in (2 * m, 2 * m + 1)
+                ]
                 first, second = (first, turned(second, swap)) if k else (turned(first, swap), second)
                 edge_rows[k, 8 * m : 8 * m + 8, lanes] = jnp.where(sub < 4, first, second)
     edge_sent[...] = edge_rows[...].astype(BF16)
@@ -437,7 +452,6 @@
 
 
 def body(state, winds, neighbours, valence, cost, w_in, w_mid, w_out):
-    vmem = pl.BlockSpec(memory_space=pltpu.VMEM)
     smem = pl.BlockSpec(memory_space=pltpu.SMEM)
     hbm = pl.BlockSpec(memory_space=pltpu.HBM)
     devices = lax.axis_size("dev")
@@ -452,9 +466,13 @@
             edge,
             edge,
         ),
-        in_specs=[smem] + [vmem] * 4 + [hbm] * 5,
+        in_specs=[smem] + [hbm] * 9,
         out_specs=[hbm] * 4,
         scratch_shapes=[
+            pltpu.VMEM((8, RIB * SWEEPS), jnp.int32),
+            pltpu.VMEM((4, RIB * SWEEPS), jnp.int32),
+            pltpu.VMEM((16, RIB * SWEEPS), jnp.int32),
+            pltpu.VMEM(TABLE.shape, F32),
             pltpu.VMEM((RIB * SWEEPS + 1, 16, 512), F32),
             pltpu.VMEM((2, RIB * SWEEPS + SWEEPS, 16, 128), F32),
             pltpu.VMEM((4, (SWEEPS + 3) * RIB * 16 + 8, 128), F32),
@@ -463,13 +481,14 @@
             pltpu.VMEM(w_in.shape, BF16),
             pltpu.VMEM((4, 384, 384), BF16),
             pltpu.VMEM(w_out.shape, BF16),
-            pltpu.VMEM((2, RIB, 8, 512), F32),
+            pltpu.VMEM((2, 3, RIB, 8, 512), F32),
             pltpu.VMEM((2, RIB * 4, 512), F32),
             pltpu.VMEM((2, RIB * 4, 512), BF16),
             pltpu.VMEM((16, RIB * SWEEPS), jnp.int32),
             pltpu.SMEM((16, RIB * SWEEPS), jnp.int32),
             pltpu.SMEM((STEPS,), jnp.int32),
             pltpu.SemaphoreType.DMA(()),
+            pltpu.SemaphoreType.DMA((4,)),
             pltpu.SemaphoreType.DMA((3,)),
             pltpu.SemaphoreType.DMA((2,)),
             pltpu.SemaphoreType.DMA((3, SWEEPS)),

time: 40.5 us -> 40.5 us (level); the launches traced: 40.9 us -> 40.1 us
  starting transfers between devices: 8.4 us -> 7.24 us
    ppermute x1, starting transfers between devices: 8.32 us -> 7.16 us  [body(): after = lax.ppermute(low, 'dev', backward)]
    pallas_call x1, Pallas kernels: 27.1 us -> 27.6 us  [body(): pl.pallas_call(main_kernel, out_shape=(jax.ShapeDtypeStruct(state.shape,...]
where the time goes in v3:
time: 40.5 us; the launch traced here: 40.1 us
  Pallas kernels  29.4 us (73%)
  starting transfers between devices  7.24 us (18%)
  waiting for transfers between devices  2.22 us (5%)
  between operations  0.66 us (2%)
  local copies, waits for them, and re-layouts  0.62 us (2%)
    pallas_call x1, Pallas kernels, body(): pl.pallas_call(main_kernel, out_shape=(jax.ShapeDtypeStruct(state.shape,...  27.6 us
    ppermute x1, starting transfers between devices, body(): after = lax.ppermute(low, 'dev', backward)  7.16 us
    ppermute x1, waiting for transfers between devices, body(): before = lax.ppermute(high, 'dev', forward)  2.15 us
    pallas_call x1, Pallas kernels, body(): pl.pallas_call(halo_kernel, out_shape=jax.ShapeDtypeStruct(state.shape, F...  1.86 us
  transfers between devices with their start and end apart: 2, of which 2 were waited for; matrix products, arithmetic and copies ran while one was open for 0% of the time, Pallas kernels for 0%

profile of v3, /device:TPU:0, one launch (start us, length us, event | category | flops | bytes accessed | tf_op | source)
XLA Modules:
  0.0 40.1 jit_solution(15801828403735002035)
XLA Ops:
  0.6 27.6 %shard_map.104 = (f32[128,16,512]{2,1,0:T(8,128)}, bf16[128,16,512]{2,1,0:T(8,128)(2,1)}, bf16[64,512]{1,0:T(8,128)(2,1)}, bf16[64,512]{1,0:T(8,128)(2,1)}) custom-call(s32[1]{0:T(128)} %bitcast.base, s32[8,128]{1,0:T(8,128)} %bitcast.5, s32[4,128]{1,0:T(4,128)} %bitcast.6, s32[16,128]{1,0:T(8,128)} %bitcast.4, f32[28,8,128]{2,1,0:T(8,128)} %constant.8.clone.table_hbm, ...), custom_call_target="tpu_custom_call" | custom-call | flops 12000000000 | bytes 14000000 | tf_op jit(solution)/shard_map/pallas_call | solution.py:461
  28.2 0.1 collective-permute-start
  28.3 7.2 %collective-permute-start.1 = (bf16[64,512]{1,0:T(8,128)(2,1)}, bf16[64,512]{1,0:T(8,128)(2,1)S(1)}, u32[]{:S(2)}, u32[]{:S(2)}) collective-permute-start(bf16[64,512]{1,0:T(8,128)(2,1)} %get-tuple-element.7), channel_id=1, source_target_pairs={{1,0},{2,1},{3,2},{4,3},{5,4},{6,5},{7,6},{8,7},{9,8},{10,9},{11,1... | collective-permute-start | bytes 196616 | tf_op jit(solution)/shard_map/ppermute | solution.py:505
  35.4 2.2 %collective-permute-done.before_hbm = bf16[64,512]{1,0:T(8,128)(2,1)S(1)} collective-permute-done((bf16[64,512]{1,0:T(8,128)(2,1)}, bf16[64,512]{1,0:T(8,128)(2,1)S(1)}, u32[]{:S(2)}, u32[]{:S(2)}) %collective-permute-start) | collective-permute-done | bytes 65568 | tf_op jit(solution)/shard_map/ppermute | solution.py:504
  37.6 0.0 copy-start
  37.6 0.1 collective-permute-done.1.after_hbm
  37.7 0.0 copy-start.1
  37.7 0.6 %copy-done = bf16[64,512]{1,0:T(8,128)(2,1)} copy-done((bf16[64,512]{1,0:T(8,128)(2,1)}, bf16[64,512]{1,0:T(8,128)(2,1)S(1)}, u32[]{:S(2)}) %copy-start) | copy-done | bytes 65560
  38.2 0.1 copy-done.1
  38.3 1.9 %shard_map.105 = f32[128,16,512]{2,1,0:T(8,128)} custom-call(bf16[64,512]{1,0:T(8,128)(2,1)} %copy-done, bf16[64,512]{1,0:T(8,128)(2,1)} %copy-done.1, f32[128,16,512]{2,1,0:T(8,128)} %get-tuple-element.8.dyn_in), custom_call_target="tpu_custom_call", output_to_operand_aliasing={{}: (2, {})} | custom-call | flops 1000000 | bytes 2000000 | tf_op jit(solution)/shard_map/pallas_call | solution.py:506
Async XLA Ops:
  28.2 9.4 %collective-permute-start = (bf16[64,512]{1,0:T(8,128)(2,1)}, bf16[64,512]{1,0:T(8,128)(2,1)S(1)}, u32[]{:S(2)}, u32[]{:S(2)}) collective-permute-start(bf16[64,512]{1,0:T(8,128)(2,1)} %get-tuple-element.6), channel_id=1, source_target_pairs={{0,1},{1,2},{2,3},{3,4},{4,5},{5,6},{6,7},{7,8},{8,9},{9,10},{10,1... | collective-permute-start | bytes 196616 | tf_op jit(solution)/shard_map/ppermute | solution.py:504
  28.3 9.4 %collective-permute-start.1 = (bf16[64,512]{1,0:T(8,128)(2,1)}, bf16[64,512]{1,0:T(8,128)(2,1)S(1)}, u32[]{:S(2)}, u32[]{:S(2)}) collective-permute-start(bf16[64,512]{1,0:T(8,128)(2,1)} %get-tuple-element.7), channel_id=1, source_target_pairs={{1,0},{2,1},{3,2},{4,3},{5,4},{6,5},{7,6},{8,7},{9,8},{10,9},{11,1... | collective-permute-start | bytes 196616 | tf_op jit(solution)/shard_map/ppermute | solution.py:505
  37.6 0.6 %copy-start = (bf16[64,512]{1,0:T(8,128)(2,1)}, bf16[64,512]{1,0:T(8,128)(2,1)S(1)}, u32[]{:S(2)}) copy-start(bf16[64,512]{1,0:T(8,128)(2,1)S(1)} %collective-permute-done.before_hbm) | copy-start | bytes 196612
  37.7 0.6 %copy-start.1 = (bf16[64,512]{1,0:T(8,128)(2,1)}, bf16[64,512]{1,0:T(8,128)(2,1)S(1)}, u32[]{:S(2)}) copy-start(bf16[64,512]{1,0:T(8,128)(2,1)S(1)} %collective-permute-done.1.after_hbm) | copy-start | bytes 196612

commit v4 on v3

--- a/solution.py
+++ b/solution.py
@@ -416,7 +416,7 @@
             copy.wait()
 
 
-def halo_kernel(before_hbm, after_hbm, dyn_in, dyn_hbm, low, high, before, after, sem):
+def halo_kernel(before, after, dyn_in, dyn_hbm, low, high, sem):
     last = RIB * (SWEEPS - 1)
     sub = sublanes()
     places = (
@@ -427,15 +427,10 @@
     stores = [
         pltpu.make_async_copy(near, far, sem.at[2 + k]) for k, (near, far) in enumerate(places)
     ]
-    arrivals = [
-        pltpu.make_async_copy(before_hbm, before, sem.at[4]),
-        pltpu.make_async_copy(after_hbm, after, sem.at[5]),
-    ]
-    for copy in loads + arrivals:
+    for copy in loads:
         copy.start()
     for k, (near, halo) in enumerate(((low, before), (high, after))):
         loads[k].wait()
-        arrivals[k].wait()
         kept = sub >= 4 if k else sub < 4
         for q in range(RIB // 4):
             packed = halo[16 * q : 16 * q + 16, :].astype(F32)
@@ -506,17 +501,15 @@
     dyn = pl.pallas_call(
         halo_kernel,
         out_shape=jax.ShapeDtypeStruct(state.shape, F32),
-        in_specs=[hbm] * 3,
+        in_specs=[pl.BlockSpec(memory_space=pltpu.VMEM)] * 2 + [hbm],
         out_specs=hbm,
         scratch_shapes=[
             pltpu.VMEM((RIB, 8, 512), F32),
             pltpu.VMEM((RIB, 8, 512), F32),
-            pltpu.VMEM((RIB * 4, 512), BF16),
-            pltpu.VMEM((RIB * 4, 512), BF16),
-            pltpu.SemaphoreType.DMA((6,)),
+            pltpu.SemaphoreType.DMA((4,)),
         ],
         input_output_aliases={2: 0},
-        compiler_params=pltpu.CompilerParams(vmem_limit_bytes=63 * 2**20),
+        compiler_params=pltpu.CompilerParams(vmem_limit_bytes=8 * 2**20),
         cost_estimate=pl.CostEstimate(
             flops=1_000_000, bytes_accessed=2_000_000, transcendentals=0
         ),

time: 40.5 us -> 39.9 us (0.985)
  local copies, waits for them, and re-layouts: 0.62 us -> 0 us
    unnamed x4 -> x0, local copies, waits for them, and re-layouts: 0.62 us -> none
where the time goes in v4:
time: 39.9 us; the launch traced here: 39.5 us
  Pallas kernels  29.4 us (74%)
  starting transfers between devices  7.24 us (18%)
  waiting for transfers between devices  2.22 us (6%)
  between operations  0.65 us (2%)
    pallas_call x1, Pallas kernels, body(): pl.pallas_call(main_kernel, out_shape=(jax.ShapeDtypeStruct(state.shape,...  27.6 us
    ppermute x1, starting transfers between devices, body(): after = lax.ppermute(low, 'dev', backward)  7.16 us
    ppermute x1, waiting for transfers between devices, body(): before = lax.ppermute(high, 'dev', forward)  2.15 us
    pallas_call x1, Pallas kernels, body(): pl.pallas_call(halo_kernel, out_shape=jax.ShapeDtypeStruct(state.shape, F...  1.8 us
  transfers between devices with their start and end apart: 2, of which 2 were waited for; matrix products, arithmetic and copies ran while one was open for 0% of the time, Pallas kernels for 0%

profile of v4, /device:TPU:0, one launch (start us, length us, event | category | flops | bytes accessed | tf_op | source)
XLA Modules:
  0.0 39.5 jit_solution(10189087514741724091)
XLA Ops:
  0.6 27.6 %shard_map.104 = (f32[128,16,512]{2,1,0:T(8,128)}, bf16[128,16,512]{2,1,0:T(8,128)(2,1)}, bf16[64,512]{1,0:T(8,128)(2,1)}, bf16[64,512]{1,0:T(8,128)(2,1)}) custom-call(s32[1]{0:T(128)} %bitcast.base, s32[8,128]{1,0:T(8,128)} %bitcast.5, s32[4,128]{1,0:T(4,128)} %bitcast.6, s32[16,128]{1,0:T(8,128)} %bitcast.4, f32[28,8,128]{2,1,0:T(8,128)} %constant.8.clone.table_hbm, ...), custom_call_target="tpu_custom_call" | custom-call | flops 12000000000 | bytes 14000000 | tf_op jit(solution)/shard_map/pallas_call | solution.py:456
  28.2 0.1 collective-permute-start
  28.3 7.2 %collective-permute-start.1 = (bf16[64,512]{1,0:T(8,128)(2,1)}, bf16[64,512]{1,0:T(8,128)(2,1)S(1)}, u32[]{:S(2)}, u32[]{:S(2)}) collective-permute-start(bf16[64,512]{1,0:T(8,128)(2,1)} %get-tuple-element.7), channel_id=1, source_target_pairs={{1,0},{2,1},{3,2},{4,3},{5,4},{6,5},{7,6},{8,7},{9,8},{10,9},{11,1... | collective-permute-start | bytes 196616 | tf_op jit(solution)/shard_map/ppermute | solution.py:500
  35.5 2.2 %collective-permute-done.before = bf16[64,512]{1,0:T(8,128)(2,1)S(1)} collective-permute-done((bf16[64,512]{1,0:T(8,128)(2,1)}, bf16[64,512]{1,0:T(8,128)(2,1)S(1)}, u32[]{:S(2)}, u32[]{:S(2)}) %collective-permute-start) | collective-permute-done | bytes 65568 | tf_op jit(solution)/shard_map/ppermute | solution.py:499
  37.6 0.1 collective-permute-done.1.after
  37.7 1.8 %shard_map.105 = f32[128,16,512]{2,1,0:T(8,128)} custom-call(bf16[64,512]{1,0:T(8,128)(2,1)S(1)} %collective-permute-done.before, bf16[64,512]{1,0:T(8,128)(2,1)S(1)} %collective-permute-done.1.after, f32[128,16,512]{2,1,0:T(8,128)} %get-tuple-element.8.dyn_in), custom_call_target="tpu_custom_call", output_to_operand_aliasing={{}: (2, {})} | custom-call | flops 1000000 | bytes 2000000 | tf_op jit(solution)/shard_map/pallas_call | solution.py:501
Async XLA Ops:
  28.2 9.4 %collective-permute-start = (bf16[64,512]{1,0:T(8,128)(2,1)}, bf16[64,512]{1,0:T(8,128)(2,1)S(1)}, u32[]{:S(2)}, u32[]{:S(2)}) collective-permute-start(bf16[64,512]{1,0:T(8,128)(2,1)} %get-tuple-element.6), channel_id=1, source_target_pairs={{0,1},{1,2},{2,3},{3,4},{4,5},{5,6},{6,7},{7,8},{8,9},{9,10},{10,1... | collective-permute-start | bytes 196616 | tf_op jit(solution)/shard_map/ppermute | solution.py:499
  28.3 9.4 %collective-permute-start.1 = (bf16[64,512]{1,0:T(8,128)(2,1)}, bf16[64,512]{1,0:T(8,128)(2,1)S(1)}, u32[]{:S(2)}, u32[]{:S(2)}) collective-permute-start(bf16[64,512]{1,0:T(8,128)(2,1)} %get-tuple-element.7), channel_id=1, source_target_pairs={{1,0},{2,1},{3,2},{4,3},{5,4},{6,5},{7,6},{8,7},{9,8},{10,9},{11,1... | collective-permute-start | bytes 196616 | tf_op jit(solution)/shard_map/ppermute | solution.py:500
